TPU v7x, 32 devices: a whole 2x2x4 slice. The times are simulated.
32 devices in a mesh: dom: 8 (over y, x, core), space: 4 (over z).
Axes of the slice: x: 2, y: 2, z: 4, core: 2. Of those that a mesh axis runs over, the one named last changes fastest.
Arguments:
- ancestor: int32 [32], replicated, may hold values from 0 to 31, as said below
- state: float32 [32, 3, 64, 2048], P('dom', None, 'space'), may hold values from -6 to 6
- jitter: float32 [32, 3, 64, 2048], P('dom', None, 'space'), may hold values from -4 to 4
- depth: float32 [64, 2048], P('space'), may hold values from 0.5 to 2
- coriolis: float32 [64, 2048], P('space'), may hold values from -1 to 1
- drag: float32 [64, 2048], P('space'), may hold values from 0.1 to 1
Outputs:
- forecast: float32 [32, 3, 64, 2048], P('dom', None, 'space')
Inputs may be any that keep to these rules, and one draw needn't show every extreme that they name: In-place replacement: every particle either keeps its slot (ancestor[j] = j) or is replaced by a survivor p with ancestor[p] = p and p != j; a survivor is the ancestor of at most two new particles. Among the particles k*4 to k*4 + 3, at most 2 are ancestors of a particle other than themselves, and in every draw some such block has exactly 2.
All inputs are finite; a program needn't handle non-finite values.
Results may differ from a plain program's by a relative error of at most 0.00007.
Values sent between devices are 32-bit elements; how exact they have to be, the bound alone decides.
A program may use at most 128 MiB of HBM per device.

v0:
```python
import jax
import jax.numpy as jnp
from jax import lax
from jax.sharding import PartitionSpec as P

STEPS = 4


time_step = 0.3


def extended(cells, sides, width):
    for axis, dim in sides:
        count = lax.axis_size(axis)
        head = lax.slice_in_dim(cells, 0, width, axis=dim)
        tail = lax.slice_in_dim(cells, cells.shape[dim] - width, cells.shape[dim], axis=dim)
        cells = jnp.concatenate(
            [
                lax.ppermute(tail, axis, [(i, (i + 1) % count) for i in range(count)]),
                cells,
                lax.ppermute(head, axis, [((i + 1) % count, i) for i in range(count)]),
            ],
            axis=dim,
        )
    return cells


def diff_zero(values):
    padded = jnp.pad(values, [(0, 0)] * (values.ndim - 1) + [(1, 1)])
    return 0.5 * (padded[..., 2:] - padded[..., :-2])


def diff_edge(values):
    padded = jnp.pad(values, [(0, 0)] * (values.ndim - 1) + [(1, 1)], mode="edge")
    return 0.5 * (padded[..., 2:] - padded[..., :-2])


def local(ancestor, state, jitter, depth, coriolis, drag):
    members = state.shape[0]
    myself = lax.axis_index("dom")
    wanted = lax.dynamic_slice_in_dim(ancestor, myself * members, members)
    piece = lax.all_gather(state, "dom", axis=0, tiled=True)
    take_count = piece.shape[0]
    select = (wanted[:, None] == jnp.arange(take_count, dtype=jnp.int32)[None, :]).astype(
        jnp.float32
    )
    copied = jnp.einsum("jk,kfrc->jfrc", select, piece, precision=lax.Precision.HIGHEST)
    fields = copied + jitter
    height, across, along = (fields[:, 0], fields[:, 1], fields[:, 2])
    for count in range(STEPS):
        flux = depth * along
        padded = extended(flux, (("space", 1),), 1)
        height_new = height - time_step * (
            diff_zero(depth * across) + 0.5 * (padded[:, 2:] - padded[:, :-2])
        )
        rimmed = extended(height_new, (("space", 1),), 1)
        across_new = (across + time_step * (coriolis * along - diff_edge(height_new))) / (
            1.0 + time_step * drag
        )
        along_new = (
            along + time_step * (-coriolis * across - 0.5 * (rimmed[:, 2:] - rimmed[:, :-2]))
        ) / (1.0 + time_step * drag)
        height, across, along = (height_new, across_new, along_new)
    return jnp.stack([height, across, along], axis=1)


def solution(mesh):
    placed = (
        P(),
        P("dom", None, "space", None),
        P("dom", None, "space", None),
        P("space", None),
        P("space", None),
        P("space", None),
    )
    return jax.shard_map(
        local, mesh=mesh, in_specs=placed, out_specs=P("dom", None, "space", None), check_vma=False
    )
```

profile of v0, /device:TPU:0, one launch (start us, length us, event | category | flops | bytes accessed | tf_op | source)
XLA Modules:
  0.0 165.9 jit_solution(18228184030796775379)
XLA Ops:
  6.5 0.0 copy-start.4
  6.5 0.0 copy-start.2
  6.5 0.0 all-gather.2.cloned.1.call-start
  6.5 0.7 all-gather.2.cloned.1.call-update
  7.3 0.0 copy-done.4
  7.3 0.1 dynamic_slice.3
  7.4 0.0 copy-start.1
  7.4 76.8 %all-gather.2.cloned.1.call-done = f32[32,3,16,2048]{3,2,1,0:T(8,128)} async-done(((f32[4,3,16,2048]{3,2,1,0:T(8,128)}), f32[32,3,16,2048]{3,2,1,0:T(8,128)}) %all-gather.2.cloned.1.call-update) | async-done | bytes 12582928 | tf_op jit(solution)/shard_map/all_gather | solution.py:42
  84.1 0.0 copy-done.2
  84.1 15.7 %fusion.2 = f32[4,3,16,2048]{3,0,2,1:T(4,128)S(1)} fusion(f32[32,3,16,2048]{3,2,1,0:T(8,128)} %all-gather.2.cloned.1.call-done, f32[4,3,16,2048]{3,2,1,0:T(8,128)S(1)} %copy-done.2, s32[4]{0:T(128)S(1)} %dynamic_slice.3), kind=kOutput, calls=%fused_computation.2 | convolution fusion | flops 151388288 | bytes 15728656 | tf_op jit(solution)/shard_map/jk,kfrc->jfrc/dot_general | solution.py:47
  99.8 0.0 copy-done.1
  99.9 0.0 copy-start.3
  99.9 0.0 copy-start
  99.9 0.2 fusion.71
  100.1 3.4 %collective-permute-start = (f32[4,1,2048]{2,0,1:T(4,128)S(1)}, f32[4,1,2048]{2,0,1:T(4,128)S(1)}, u32[]{:S(2)}, u32[]{:S(2)}) collective-permute-start(f32[4,1,2048]{2,0,1:T(4,128)S(1)} %get-tuple-element.49), channel_id=1, source_target_pairs={{1,0},{2,1},{3,2},{0,3},{5,4},{6,5},{7,6},{4,7},{9,8},{10,9},{11,1... | collective-permute-start | bytes 98312 | tf_op jit(solution)/shard_map/ppermute | solution.py:21
  103.5 0.0 collective-permute-start.1
  103.5 0.0 copy-done.3
  103.6 0.0 copy-done
  103.6 1.5 collective-permute-done
  105.1 4.1 %collective-permute-done.1 = f32[4,1,2048]{2,0,1:T(4,128)S(1)} collective-permute-done((f32[4,1,2048]{2,0,1:T(4,128)S(1)}, f32[4,1,2048]{2,0,1:T(4,128)S(1)}, u32[]{:S(2)}, u32[]{:S(2)}) %collective-permute-start.1) | collective-permute-done | bytes 32800 | tf_op jit(solution)/shard_map/ppermute | solution.py:19
  109.2 0.6 fusion.68
  109.9 0.1 collective-permute-start.2
  109.9 2.0 %collective-permute-start.3 = (f32[4,1,2048]{2,0,1:T(4,128)S(1)}, f32[4,1,2048]{2,0,1:T(4,128)S(1)}, u32[]{:S(2)}, u32[]{:S(2)}) collective-permute-start(f32[4,1,2048]{2,0,1:T(4,128)S(1)} %get-tuple-element.48), channel_id=1, source_target_pairs={{0,1},{1,2},{2,3},{3,0},{4,5},{5,6},{6,7},{7,4},{8,9},{9,10},{10,1... | collective-permute-start | bytes 98312 | tf_op jit(solution)/shard_map/ppermute | solution.py:19
  112.0 0.1 fusion.90
  112.0 1.9 %collective-permute-done.2 = f32[4,1,2048]{2,0,1:T(4,128)S(1)} collective-permute-done((f32[4,1,2048]{2,0,1:T(4,128)S(1)}, f32[4,1,2048]{2,0,1:T(4,128)S(1)}, u32[]{:S(2)}, u32[]{:S(2)}) %collective-permute-start.2) | collective-permute-done | bytes 32800 | tf_op jit(solution)/shard_map/ppermute | solution.py:21
  113.9 1.8 %collective-permute-done.3 = f32[4,1,2048]{2,0,1:T(4,128)S(1)} collective-permute-done((f32[4,1,2048]{2,0,1:T(4,128)S(1)}, f32[4,1,2048]{2,0,1:T(4,128)S(1)}, u32[]{:S(2)}, u32[]{:S(2)}) %collective-permute-start.3) | collective-permute-done | bytes 32800 | tf_op jit(solution)/shard_map/ppermute | solution.py:19
  115.7 0.9 broadcast_multiply_fusion.5
  116.6 0.1 collective-permute-start.4
  116.7 2.0 %collective-permute-start.5 = (f32[4,1,2048]{2,0,1:T(4,128)S(1)}, f32[4,1,2048]{2,0,1:T(4,128)S(1)}, u32[]{:S(2)}, u32[]{:S(2)}) collective-permute-start(f32[4,1,2048]{2,0,1:T(4,128)S(1)} %get-tuple-element.46), channel_id=1, source_target_pairs={{0,1},{1,2},{2,3},{3,0},{4,5},{5,6},{6,7},{7,4},{8,9},{9,10},{10,1... | collective-permute-start | bytes 98312 | tf_op jit(solution)/shard_map/ppermute | solution.py:19
  118.7 1.9 %collective-permute-done.4 = f32[4,1,2048]{2,0,1:T(4,128)S(1)} collective-permute-done((f32[4,1,2048]{2,0,1:T(4,128)S(1)}, f32[4,1,2048]{2,0,1:T(4,128)S(1)}, u32[]{:S(2)}, u32[]{:S(2)}) %collective-permute-start.4) | collective-permute-done | bytes 32800 | tf_op jit(solution)/shard_map/ppermute | solution.py:21
  120.6 1.9 %collective-permute-done.5 = f32[4,1,2048]{2,0,1:T(4,128)S(1)} collective-permute-done((f32[4,1,2048]{2,0,1:T(4,128)S(1)}, f32[4,1,2048]{2,0,1:T(4,128)S(1)}, u32[]{:S(2)}, u32[]{:S(2)}) %collective-permute-start.5) | collective-permute-done | bytes 32800 | tf_op jit(solution)/shard_map/ppermute | solution.py:19
  122.5 0.6 fusion.52
  123.1 0.1 collective-permute-start.6
  123.2 2.0 %collective-permute-start.7 = (f32[4,1,2048]{2,0,1:T(4,128)S(1)}, f32[4,1,2048]{2,0,1:T(4,128)S(1)}, u32[]{:S(2)}, u32[]{:S(2)}) collective-permute-start(f32[4,1,2048]{2,0,1:T(4,128)S(1)} %get-tuple-element.42), channel_id=1, source_target_pairs={{0,1},{1,2},{2,3},{3,0},{4,5},{5,6},{6,7},{7,4},{8,9},{9,10},{10,1... | collective-permute-start | bytes 98312 | tf_op jit(solution)/shard_map/ppermute | solution.py:19
  125.2 0.1 fusion.87
  125.3 1.8 %collective-permute-done.6 = f32[4,1,2048]{2,0,1:T(4,128)S(1)} collective-permute-done((f32[4,1,2048]{2,0,1:T(4,128)S(1)}, f32[4,1,2048]{2,0,1:T(4,128)S(1)}, u32[]{:S(2)}, u32[]{:S(2)}) %collective-permute-start.6) | collective-permute-done | bytes 32800 | tf_op jit(solution)/shard_map/ppermute | solution.py:21
  127.1 1.9 %collective-permute-done.7 = f32[4,1,2048]{2,0,1:T(4,128)S(1)} collective-permute-done((f32[4,1,2048]{2,0,1:T(4,128)S(1)}, f32[4,1,2048]{2,0,1:T(4,128)S(1)}, u32[]{:S(2)}, u32[]{:S(2)}) %collective-permute-start.7) | collective-permute-done | bytes 32800 | tf_op jit(solution)/shard_map/ppermute | solution.py:19
  129.0 1.0 broadcast_multiply_fusion.3
  129.9 0.1 collective-permute-start.8
  130.0 2.0 %collective-permute-start.9 = (f32[4,1,2048]{2,0,1:T(4,128)S(1)}, f32[4,1,2048]{2,0,1:T(4,128)S(1)}, u32[]{:S(2)}, u32[]{:S(2)}) collective-permute-start(f32[4,1,2048]{2,0,1:T(4,128)S(1)} %get-tuple-element.40), channel_id=1, source_target_pairs={{0,1},{1,2},{2,3},{3,0},{4,5},{5,6},{6,7},{7,4},{8,9},{9,10},{10,1... | collective-permute-start | bytes 98312 | tf_op jit(solution)/shard_map/ppermute | solution.py:19
  132.0 2.1 %collective-permute-done.8 = f32[4,1,2048]{2,0,1:T(4,128)S(1)} collective-permute-done((f32[4,1,2048]{2,0,1:T(4,128)S(1)}, f32[4,1,2048]{2,0,1:T(4,128)S(1)}, u32[]{:S(2)}, u32[]{:S(2)}) %collective-permute-start.8) | collective-permute-done | bytes 32800 | tf_op jit(solution)/shard_map/ppermute | solution.py:21
  134.1 1.9 %collective-permute-done.9 = f32[4,1,2048]{2,0,1:T(4,128)S(1)} collective-permute-done((f32[4,1,2048]{2,0,1:T(4,128)S(1)}, f32[4,1,2048]{2,0,1:T(4,128)S(1)}, u32[]{:S(2)}, u32[]{:S(2)}) %collective-permute-start.9) | collective-permute-done | bytes 32800 | tf_op jit(solution)/shard_map/ppermute | solution.py:19
  136.0 0.6 fusion.36
  136.6 0.1 collective-permute-start.10
  136.7 2.0 %collective-permute-start.11 = (f32[4,1,2048]{2,0,1:T(4,128)S(1)}, f32[4,1,2048]{2,0,1:T(4,128)S(1)}, u32[]{:S(2)}, u32[]{:S(2)}) collective-permute-start(f32[4,1,2048]{2,0,1:T(4,128)S(1)} %get-tuple-element.36), channel_id=1, source_target_pairs={{0,1},{1,2},{2,3},{3,0},{4,5},{5,6},{6,7},{7,4},{8,9},{9,10},{10,1... | collective-permute-start | bytes 98312 | tf_op jit(solution)/shard_map/ppermute | solution.py:19
  138.7 0.1 fusion.84
  138.8 1.8 %collective-permute-done.10 = f32[4,1,2048]{2,0,1:T(4,128)S(1)} collective-permute-done((f32[4,1,2048]{2,0,1:T(4,128)S(1)}, f32[4,1,2048]{2,0,1:T(4,128)S(1)}, u32[]{:S(2)}, u32[]{:S(2)}) %collective-permute-start.10) | collective-permute-done | bytes 32800 | tf_op jit(solution)/shard_map/ppermute | solution.py:21
  140.6 1.9 %collective-permute-done.11 = f32[4,1,2048]{2,0,1:T(4,128)S(1)} collective-permute-done((f32[4,1,2048]{2,0,1:T(4,128)S(1)}, f32[4,1,2048]{2,0,1:T(4,128)S(1)}, u32[]{:S(2)}, u32[]{:S(2)}) %collective-permute-start.11) | collective-permute-done | bytes 32800 | tf_op jit(solution)/shard_map/ppermute | solution.py:19
  142.5 1.0 broadcast_multiply_fusion.1
  143.4 0.2 collective-permute-start.12
  143.6 1.9 %collective-permute-start.13 = (f32[4,1,2048]{2,0,1:T(4,128)S(1)}, f32[4,1,2048]{2,0,1:T(4,128)S(1)}, u32[]{:S(2)}, u32[]{:S(2)}) collective-permute-start(f32[4,1,2048]{2,0,1:T(4,128)S(1)} %get-tuple-element.34), channel_id=1, source_target_pairs={{0,1},{1,2},{2,3},{3,0},{4,5},{5,6},{6,7},{7,4},{8,9},{9,10},{10,1... | collective-permute-start | bytes 98312 | tf_op jit(solution)/shard_map/ppermute | solution.py:19
  145.5 1.9 %collective-permute-done.12 = f32[4,1,2048]{2,0,1:T(4,128)S(1)} collective-permute-done((f32[4,1,2048]{2,0,1:T(4,128)S(1)}, f32[4,1,2048]{2,0,1:T(4,128)S(1)}, u32[]{:S(2)}, u32[]{:S(2)}) %collective-permute-start.12) | collective-permute-done | bytes 32800 | tf_op jit(solution)/shard_map/ppermute | solution.py:21
  147.4 1.9 %collective-permute-done.13 = f32[4,1,2048]{2,0,1:T(4,128)S(1)} collective-permute-done((f32[4,1,2048]{2,0,1:T(4,128)S(1)}, f32[4,1,2048]{2,0,1:T(4,128)S(1)}, u32[]{:S(2)}, u32[]{:S(2)}) %collective-permute-start.13) | collective-permute-done | bytes 32800 | tf_op jit(solution)/shard_map/ppermute | solution.py:19
  149.3 0.6 fusion.20
  150.0 0.1 collective-permute-start.14
  150.0 2.0 %collective-permute-start.15 = (f32[4,1,2048]{2,0,1:T(4,128)S(1)}, f32[4,1,2048]{2,0,1:T(4,128)S(1)}, u32[]{:S(2)}, u32[]{:S(2)}) collective-permute-start(f32[4,1,2048]{2,0,1:T(4,128)S(1)} %get-tuple-element.30), channel_id=1, source_target_pairs={{0,1},{1,2},{2,3},{3,0},{4,5},{5,6},{6,7},{7,4},{8,9},{9,10},{10,1... | collective-permute-start | bytes 98312 | tf_op jit(solution)/shard_map/ppermute | solution.py:19
  152.0 0.1 fusion.82
  152.1 1.8 %collective-permute-done.14 = f32[4,1,2048]{2,0,1:T(4,128)S(1)} collective-permute-done((f32[4,1,2048]{2,0,1:T(4,128)S(1)}, f32[4,1,2048]{2,0,1:T(4,128)S(1)}, u32[]{:S(2)}, u32[]{:S(2)}) %collective-permute-start.14) | collective-permute-done | bytes 32800 | tf_op jit(solution)/shard_map/ppermute | solution.py:21
  153.9 1.9 %collective-permute-done.15 = f32[4,1,2048]{2,0,1:T(4,128)S(1)} collective-permute-done((f32[4,1,2048]{2,0,1:T(4,128)S(1)}, f32[4,1,2048]{2,0,1:T(4,128)S(1)}, u32[]{:S(2)}, u32[]{:S(2)}) %collective-permute-start.15) | collective-permute-done | bytes 32800 | tf_op jit(solution)/shard_map/ppermute | solution.py:19
  155.8 0.8 fusion.69
  156.6 0.4 pad_maximum_fusion
  157.0 2.1 %copy.12 = f32[4,3,16,2048]{3,2,1,0:T(8,128)} copy(f32[4,3,16,2048]{3,0,2,1:T(4,128)S(1)} %pad_maximum_fusion) | data formatting | bytes 3145728 | tf_op jit(solution)/shard_map/stack | solution.py:64
  (10 shorter events, 0.1 us)
Async XLA Ops:
  6.5 0.7 copy-start.4
  6.5 77.6 %copy-start.2 = (f32[4,3,16,2048]{3,2,1,0:T(8,128)S(1)}, f32[4,3,16,2048]{3,2,1,0:T(8,128)}, u32[]{:S(2)}) copy-start(f32[4,3,16,2048]{3,2,1,0:T(8,128)} %param.8) | copy-start | bytes 4718596
  6.5 77.6 %all-gather.2.cloned.1.call-start = ((), (), s32[]{:S(2)}) async-start(), calls=%async_computation | async-start | bytes 14155776 | tf_op jit(solution)/shard_map/all_gather | solution.py:42
  7.4 92.5 %copy-start.1 = (f32[16,2048]{1,0:T(8,128)S(1)}, f32[16,2048]{1,0:T(8,128)}, u32[]{:S(2)}) copy-start(f32[16,2048]{1,0:T(8,128)} %param.9) | copy-start | bytes 393220
  99.9 3.7 %copy-start.3 = (f32[16,2048]{1,0:T(8,128)S(1)}, f32[16,2048]{1,0:T(8,128)}, u32[]{:S(2)}) copy-start(f32[16,2048]{1,0:T(8,128)} %param.11) | copy-start | bytes 393220
  99.9 3.7 %copy-start = (f32[16,2048]{1,0:T(8,128)S(1)}, f32[16,2048]{1,0:T(8,128)}, u32[]{:S(2)}) copy-start(f32[16,2048]{1,0:T(8,128)} %param.10) | copy-start | bytes 393220
  100.1 5.0 %collective-permute-start = (f32[4,1,2048]{2,0,1:T(4,128)S(1)}, f32[4,1,2048]{2,0,1:T(4,128)S(1)}, u32[]{:S(2)}, u32[]{:S(2)}) collective-permute-start(f32[4,1,2048]{2,0,1:T(4,128)S(1)} %get-tuple-element.49), channel_id=1, source_target_pairs={{1,0},{2,1},{3,2},{0,3},{5,4},{6,5},{7,6},{4,7},{9,8},{10,9},{11,1... | collective-permute-start | bytes 98312 | tf_op jit(solution)/shard_map/ppermute | solution.py:21
  103.5 5.7 %collective-permute-start.1 = (f32[4,1,2048]{2,0,1:T(4,128)S(1)}, f32[4,1,2048]{2,0,1:T(4,128)S(1)}, u32[]{:S(2)}, u32[]{:S(2)}) collective-permute-start(f32[4,1,2048]{2,0,1:T(4,128)S(1)} %get-tuple-element.50), channel_id=1, source_target_pairs={{0,1},{1,2},{2,3},{3,0},{4,5},{5,6},{6,7},{7,4},{8,9},{9,10},{10,1... | collective-permute-start | bytes 98312 | tf_op jit(solution)/shard_map/ppermute | solution.py:19
  109.9 4.0 %collective-permute-start.2 = (f32[4,1,2048]{2,0,1:T(4,128)S(1)}, f32[4,1,2048]{2,0,1:T(4,128)S(1)}, u32[]{:S(2)}, u32[]{:S(2)}) collective-permute-start(f32[4,1,2048]{2,0,1:T(4,128)S(1)} %get-tuple-element.47), channel_id=1, source_target_pairs={{1,0},{2,1},{3,2},{0,3},{5,4},{6,5},{7,6},{4,7},{9,8},{10,9},{11,1... | collective-permute-start | bytes 98312 | tf_op jit(solution)/shard_map/ppermute | solution.py:21
  109.9 5.8 %collective-permute-start.3 = (f32[4,1,2048]{2,0,1:T(4,128)S(1)}, f32[4,1,2048]{2,0,1:T(4,128)S(1)}, u32[]{:S(2)}, u32[]{:S(2)}) collective-permute-start(f32[4,1,2048]{2,0,1:T(4,128)S(1)} %get-tuple-element.48), channel_id=1, source_target_pairs={{0,1},{1,2},{2,3},{3,0},{4,5},{5,6},{6,7},{7,4},{8,9},{9,10},{10,1... | collective-permute-start | bytes 98312 | tf_op jit(solution)/shard_map/ppermute | solution.py:19
  116.6 4.0 %collective-permute-start.4 = (f32[4,1,2048]{2,0,1:T(4,128)S(1)}, f32[4,1,2048]{2,0,1:T(4,128)S(1)}, u32[]{:S(2)}, u32[]{:S(2)}) collective-permute-start(f32[4,1,2048]{2,0,1:T(4,128)S(1)} %get-tuple-element.45), channel_id=1, source_target_pairs={{1,0},{2,1},{3,2},{0,3},{5,4},{6,5},{7,6},{4,7},{9,8},{10,9},{11,1... | collective-permute-start | bytes 98312 | tf_op jit(solution)/shard_map/ppermute | solution.py:21
  116.7 5.8 %collective-permute-start.5 = (f32[4,1,2048]{2,0,1:T(4,128)S(1)}, f32[4,1,2048]{2,0,1:T(4,128)S(1)}, u32[]{:S(2)}, u32[]{:S(2)}) collective-permute-start(f32[4,1,2048]{2,0,1:T(4,128)S(1)} %get-tuple-element.46), channel_id=1, source_target_pairs={{0,1},{1,2},{2,3},{3,0},{4,5},{5,6},{6,7},{7,4},{8,9},{9,10},{10,1... | collective-permute-start | bytes 98312 | tf_op jit(solution)/shard_map/ppermute | solution.py:19
  123.1 4.0 %collective-permute-start.6 = (f32[4,1,2048]{2,0,1:T(4,128)S(1)}, f32[4,1,2048]{2,0,1:T(4,128)S(1)}, u32[]{:S(2)}, u32[]{:S(2)}) collective-permute-start(f32[4,1,2048]{2,0,1:T(4,128)S(1)} %get-tuple-element.41), channel_id=1, source_target_pairs={{1,0},{2,1},{3,2},{0,3},{5,4},{6,5},{7,6},{4,7},{9,8},{10,9},{11,1... | collective-permute-start | bytes 98312 | tf_op jit(solution)/shard_map/ppermute | solution.py:21
  123.2 5.8 %collective-permute-start.7 = (f32[4,1,2048]{2,0,1:T(4,128)S(1)}, f32[4,1,2048]{2,0,1:T(4,128)S(1)}, u32[]{:S(2)}, u32[]{:S(2)}) collective-permute-start(f32[4,1,2048]{2,0,1:T(4,128)S(1)} %get-tuple-element.42), channel_id=1, source_target_pairs={{0,1},{1,2},{2,3},{3,0},{4,5},{5,6},{6,7},{7,4},{8,9},{9,10},{10,1... | collective-permute-start | bytes 98312 | tf_op jit(solution)/shard_map/ppermute | solution.py:19
  129.9 4.2 %collective-permute-start.8 = (f32[4,1,2048]{2,0,1:T(4,128)S(1)}, f32[4,1,2048]{2,0,1:T(4,128)S(1)}, u32[]{:S(2)}, u32[]{:S(2)}) collective-permute-start(f32[4,1,2048]{2,0,1:T(4,128)S(1)} %get-tuple-element.39), channel_id=1, source_target_pairs={{1,0},{2,1},{3,2},{0,3},{5,4},{6,5},{7,6},{4,7},{9,8},{10,9},{11,1... | collective-permute-start | bytes 98312 | tf_op jit(solution)/shard_map/ppermute | solution.py:21
  130.0 6.0 %collective-permute-start.9 = (f32[4,1,2048]{2,0,1:T(4,128)S(1)}, f32[4,1,2048]{2,0,1:T(4,128)S(1)}, u32[]{:S(2)}, u32[]{:S(2)}) collective-permute-start(f32[4,1,2048]{2,0,1:T(4,128)S(1)} %get-tuple-element.40), channel_id=1, source_target_pairs={{0,1},{1,2},{2,3},{3,0},{4,5},{5,6},{6,7},{7,4},{8,9},{9,10},{10,1... | collective-permute-start | bytes 98312 | tf_op jit(solution)/shard_map/ppermute | solution.py:19
  136.6 4.0 %collective-permute-start.10 = (f32[4,1,2048]{2,0,1:T(4,128)S(1)}, f32[4,1,2048]{2,0,1:T(4,128)S(1)}, u32[]{:S(2)}, u32[]{:S(2)}) collective-permute-start(f32[4,1,2048]{2,0,1:T(4,128)S(1)} %get-tuple-element.35), channel_id=1, source_target_pairs={{1,0},{2,1},{3,2},{0,3},{5,4},{6,5},{7,6},{4,7},{9,8},{10,9},{11,1... | collective-permute-start | bytes 98312 | tf_op jit(solution)/shard_map/ppermute | solution.py:21
  136.7 5.8 %collective-permute-start.11 = (f32[4,1,2048]{2,0,1:T(4,128)S(1)}, f32[4,1,2048]{2,0,1:T(4,128)S(1)}, u32[]{:S(2)}, u32[]{:S(2)}) collective-permute-start(f32[4,1,2048]{2,0,1:T(4,128)S(1)} %get-tuple-element.36), channel_id=1, source_target_pairs={{0,1},{1,2},{2,3},{3,0},{4,5},{5,6},{6,7},{7,4},{8,9},{9,10},{10,1... | collective-permute-start | bytes 98312 | tf_op jit(solution)/shard_map/ppermute | solution.py:19
  143.4 4.0 %collective-permute-start.12 = (f32[4,1,2048]{2,0,1:T(4,128)S(1)}, f32[4,1,2048]{2,0,1:T(4,128)S(1)}, u32[]{:S(2)}, u32[]{:S(2)}) collective-permute-start(f32[4,1,2048]{2,0,1:T(4,128)S(1)} %get-tuple-element.33), channel_id=1, source_target_pairs={{1,0},{2,1},{3,2},{0,3},{5,4},{6,5},{7,6},{4,7},{9,8},{10,9},{11,1... | collective-permute-start | bytes 98312 | tf_op jit(solution)/shard_map/ppermute | solution.py:21
  143.6 5.7 %collective-permute-start.13 = (f32[4,1,2048]{2,0,1:T(4,128)S(1)}, f32[4,1,2048]{2,0,1:T(4,128)S(1)}, u32[]{:S(2)}, u32[]{:S(2)}) collective-permute-start(f32[4,1,2048]{2,0,1:T(4,128)S(1)} %get-tuple-element.34), channel_id=1, source_target_pairs={{0,1},{1,2},{2,3},{3,0},{4,5},{5,6},{6,7},{7,4},{8,9},{9,10},{10,1... | collective-permute-start | bytes 98312 | tf_op jit(solution)/shard_map/ppermute | solution.py:19
  150.0 4.0 %collective-permute-start.14 = (f32[4,1,2048]{2,0,1:T(4,128)S(1)}, f32[4,1,2048]{2,0,1:T(4,128)S(1)}, u32[]{:S(2)}, u32[]{:S(2)}) collective-permute-start(f32[4,1,2048]{2,0,1:T(4,128)S(1)} %get-tuple-element.29), channel_id=1, source_target_pairs={{1,0},{2,1},{3,2},{0,3},{5,4},{6,5},{7,6},{4,7},{9,8},{10,9},{11,1... | collective-permute-start | bytes 98312 | tf_op jit(solution)/shard_map/ppermute | solution.py:21
  150.0 5.8 %collective-permute-start.15 = (f32[4,1,2048]{2,0,1:T(4,128)S(1)}, f32[4,1,2048]{2,0,1:T(4,128)S(1)}, u32[]{:S(2)}, u32[]{:S(2)}) collective-permute-start(f32[4,1,2048]{2,0,1:T(4,128)S(1)} %get-tuple-element.30), channel_id=1, source_target_pairs={{0,1},{1,2},{2,3},{3,0},{4,5},{5,6},{6,7},{7,4},{8,9},{9,10},{10,1... | collective-permute-start | bytes 98312 | tf_op jit(solution)/shard_map/ppermute | solution.py:19
Sparse Core Ops, SparseCore 0:
  9.3 74.8 all-gather.1
where the time goes:
time: 166 us
  waiting for transfers between devices  109 us (66%)
  starting transfers between devices  17.9 us (11%)
  matrix products  15.7 us (9%)
  between operations  13.6 us (8%)
  other arithmetic  6.77 us (4%)
  local copies, waits for them, and re-layouts  2.54 us (2%)
    all_gather x1, waiting for transfers between devices, local(): piece = lax.all_gather(state, 'dom', axis=0, tiled=True)  76.8 us
    ppermute x8, waiting for transfers between devices, extended(): lax.ppermute(tail, axis, [(i, (i + 1) % count) for i in range(count)])  17.2 us
    dot_general x1, matrix products, local(): jnp.einsum('jk,kfrc->jfrc', select, piece, precision=lax.Precision.HIGHEST)  15.7 us
    ppermute x8, waiting for transfers between devices, extended(): lax.ppermute(head, axis, [((i + 1) % count, i) for i in range(count)])  14.7 us
    ppermute x8, starting transfers between devices, extended(): lax.ppermute(tail, axis, [(i, (i + 1) % count) for i in range(count)])  14 us
    ppermute x8, starting transfers between devices, extended(): lax.ppermute(head, axis, [((i + 1) % count, i) for i in range(count)])  3.91 us
  transfers between devices with their start and end apart: 17, of which 17 were waited for; matrix products, arithmetic and copies ran while one was open for 0% of the time, Pallas kernels for 0%

commit v1 on v0

v1 whole, which is shorter than its diff:
```python
import functools

import jax
import jax.numpy as jnp
from jax import lax
from jax.experimental import pallas as pl
from jax.experimental.pallas import tpu as pltpu
from jax.sharding import PartitionSpec as P

STEPS = 4
DT = 0.3
CAP = 2
MESH = pl.DeviceIdType.MESH
UP, DOWN = 0, 1


def column_difference(a, edge):
    width = a.shape[1]
    column = lax.broadcasted_iota(jnp.int32, a.shape, 1)
    beyond = a if edge else jnp.zeros_like(a)
    after = jnp.where(column == width - 1, beyond, pltpu.roll(a, width - 1, 1))
    before = jnp.where(column == 0, beyond, pltpu.roll(a, 1, 1))
    return after - before


def row_difference(a, above, below):
    rows = a.shape[0]
    row = lax.broadcasted_iota(jnp.int32, a.shape, 0)
    after = jnp.where(row == rows - 1, below, pltpu.roll(a, rows - 1, 0))
    before = jnp.where(row == 0, above, pltpu.roll(a, 1, 0))
    return after - before


def advance_kernel(
    count, groups,
    copied, jitter, depth, coriolis, drag, out,
    flux_c, keep_c, turn_c, push_c, rim_send, rim_recv, send, recv, last_send, last_recv, halo,
    send_sem, recv_sem,
):
    members, _, rows, width = out.shape
    each = members // groups
    me = lax.axis_index("space")
    above, below = lax.rem(me + count - 1, count), lax.rem(me + 1, count)
    towards = (above, below)

    barrier = pltpu.get_barrier_semaphore()
    for neighbour in towards:
        pl.semaphore_signal(barrier, inc=1, device_id={"space": neighbour}, device_id_type=MESH)

    def exchange(number, source, target, side):
        return pltpu.make_async_remote_copy(
            src_ref=source, dst_ref=target,
            send_sem=send_sem.at[number, side], recv_sem=recv_sem.at[number, 1 - side],
            device_id={"space": towards[side]}, device_id_type=MESH,
        )

    def rim(side):
        return exchange(0, rim_send.at[side], rim_recv.at[1 - side], side)

    def swap(step, group, side):
        number = 1 + step * groups + group
        if step == STEPS:
            return exchange(number, last_send.at[group, side], last_recv.at[group, 1 - side], side)
        return exchange(number, send.at[step, group, side], recv.at[step, group, 1 - side], side)

    for side, row in ((UP, 0), (DOWN, rows - 1)):
        for k, plane in enumerate((depth, coriolis, drag, drag)):
            rim_send[side, k : k + 1, :] = plane[row : row + 1, :]
        for group in range(groups):
            for i in range(each):
                p = group * each + i
                for k, part in enumerate((1, 2)):
                    send[0, group, side, k * each + i : k * each + i + 1, :] = (
                        copied[p, part, row : row + 1, :] + jitter[p, part, row : row + 1, :]
                    )
    pl.semaphore_wait(barrier, 2)
    for side in (UP, DOWN):
        rim(side).start()
    for group in range(groups):
        for side in (UP, DOWN):
            swap(0, group, side).start()

    keep = 1.0 / (1.0 + DT * drag[...])
    flux_c[...] = 0.5 * DT * depth[...]
    keep_c[...] = keep
    turn_c[...] = DT * coriolis[...] * keep
    push_c[...] = 0.5 * DT * keep
    for p in range(members):
        out[p] = copied[p] + jitter[p]
    for side in (UP, DOWN):
        rim(side).wait_recv()
    edge = []
    for side in (UP, DOWN):
        k = 1.0 / (1.0 + DT * rim_recv[side, 2:3, :])
        edge.append(
            (0.5 * DT * rim_recv[side, 0:1, :], k, DT * rim_recv[side, 1:2, :] * k, 0.5 * DT * k)
        )
    for side in (UP, DOWN):
        for k in range(4):
            rim_recv[side, k : k + 1, :] = edge[side][k]

    def finish(step, group):
        for side in (UP, DOWN):
            swap(step, group, side).wait_recv()
        for i in range(each):
            p = group * each + i
            if step == STEPS:
                up, down = last_recv[group, UP, i : i + 1, :], last_recv[group, DOWN, i : i + 1, :]
            else:
                up, down = recv[step, group, UP, i : i + 1, :], recv[step, group, DOWN, i : i + 1, :]
            height = out[p, 0]
            out[p, 2] = out[p, 2] - push_c[...] * row_difference(height, up, down)
            if step == STEPS:
                continue
            for side, near, own in ((UP, up, height[0:1, :]), (DOWN, down, height[rows - 1 : rows, :])):
                far = recv[step, group, side, each + i : each + i + 1, :]
                k, t, b = (rim_recv[side, n : n + 1, :] for n in (1, 2, 3))
                u, v = halo[p, side, 0:1, :], halo[p, side, 1:2, :]
                across = own - far if side == UP else far - own
                halo[p, side, 0:1, :] = u * k + t * v - b * column_difference(near, True)
                halo[p, side, 1:2, :] = v * k - t * u - b * across

    for step in range(1, STEPS + 1):
        for group in range(groups):
            if step == 1:
                for side in (UP, DOWN):
                    swap(0, group, side).wait_recv()
                for side in (UP, DOWN):
                    for i in range(each):
                        for k in range(2):
                            halo[group * each + i, side, k : k + 1, :] = recv[
                                0, group, side, k * each + i : k * each + i + 1, :
                            ]
            else:
                finish(step - 1, group)
            for i in range(each):
                p = group * each + i
                u, v = out[p, 1], out[p, 2]
                f = flux_c[...]
                height = out[p, 0] - (
                    column_difference(f * u, False)
                    + row_difference(
                        f * v,
                        rim_recv[UP, 0:1, :] * halo[p, UP, 1:2, :],
                        rim_recv[DOWN, 0:1, :] * halo[p, DOWN, 1:2, :],
                    )
                )
                out[p, 0] = height
                if step == STEPS:
                    last_send[group, UP, i : i + 1, :] = height[0:1, :]
                    last_send[group, DOWN, i : i + 1, :] = height[rows - 1 : rows, :]
                else:
                    for k in range(2):
                        at = slice(k * each + i, k * each + i + 1)
                        send[step, group, UP, at, :] = height[k : k + 1, :]
                        send[step, group, DOWN, at, :] = height[rows - 1 - k : rows - k, :]
            for side in (UP, DOWN):
                swap(step, group, side).start()
            for i in range(each):
                p = group * each + i
                u, v = out[p, 1], out[p, 2]
                out[p, 1] = u * keep_c[...] + turn_c[...] * v - push_c[...] * column_difference(out[p, 0], True)
                out[p, 2] = v * keep_c[...] - turn_c[...] * u
    for group in range(groups):
        finish(STEPS, group)
    for side in (UP, DOWN):
        rim(side).wait_send()
        for step in range(STEPS + 1):
            for group in range(groups):
                swap(step, group, side).wait_send()


def advance(copied, jitter, depth, coriolis, drag, count):
    members, _, rows, width = jitter.shape
    groups = 2
    each = members // groups
    f32 = jnp.float32
    plane = pltpu.VMEM((rows, width), f32)
    copies = 1 + (STEPS + 1) * groups
    return pl.pallas_call(
        functools.partial(advance_kernel, count, groups),
        out_shape=jax.ShapeDtypeStruct(jitter.shape, f32),
        in_specs=[pl.BlockSpec(memory_space=pltpu.VMEM)] * 5,
        out_specs=pl.BlockSpec(memory_space=pltpu.VMEM),
        scratch_shapes=[
            plane, plane, plane, plane,
            pltpu.VMEM((2, 4, width), f32),
            pltpu.VMEM((2, 4, width), f32),
            pltpu.VMEM((STEPS, groups, 2, 2 * each, width), f32),
            pltpu.VMEM((STEPS, groups, 2, 2 * each, width), f32),
            pltpu.VMEM((groups, 2, each, width), f32),
            pltpu.VMEM((groups, 2, each, width), f32),
            pltpu.VMEM((members, 2, 2, width), f32),
            pltpu.SemaphoreType.DMA((copies, 2)),
            pltpu.SemaphoreType.DMA((copies, 2)),
        ],
        compiler_params=pltpu.CompilerParams(
            collective_id=0, has_side_effects=True, vmem_limit_bytes=40 * 1024 * 1024
        ),
        name="advance",
    )(copied, jitter, depth, coriolis, drag)


def local(count, ancestor, state, jitter, depth, coriolis, drag):
    members = state.shape[0]
    part = ancestor.shape[0]
    first = lax.axis_index("dom") * members
    index = jnp.arange(part, dtype=jnp.int32)
    moved = ancestor != index
    donor = jnp.any((ancestor[:, None] == index[None, :]) & moved[:, None], axis=0)
    earlier = (index[None, :] < index[:, None]) & (index[None, :] // members == index[:, None] // members)
    place = jnp.sum((earlier & donor[None, :]).astype(jnp.int32), axis=1)
    sent = []
    for k in range(CAP):
        hit = donor & (place == k) & (index // members == first // members)
        slot = jnp.sum(jnp.where(hit, index - first, 0))
        sent.append(lax.dynamic_slice_in_dim(state, slot, 1))
    pool = lax.all_gather(jnp.concatenate(sent), "dom", axis=0, tiled=True)
    where = (ancestor // members) * CAP + jnp.sum(
        jnp.where(ancestor[:, None] == index[None, :], place[None, :], 0), axis=1
    )
    copied = []
    for k in range(members):
        j = first + k
        got = lax.dynamic_slice_in_dim(pool, where[j], 1)
        copied.append(jnp.where(moved[j], got, state[k : k + 1]))
    return advance(jnp.concatenate(copied), jitter, depth, coriolis, drag, count)


def solution(mesh):
    field = P("dom", None, "space", None)
    plane = P("space", None)
    return jax.shard_map(
        functools.partial(local, mesh.shape["space"]),
        mesh=mesh,
        in_specs=(P(), field, field, plane, plane, plane),
        out_specs=field,
        check_vma=False,
    )
```

time: 166 us -> 106 us (0.64)
  waiting for transfers between devices: 109 us -> 39.7 us
  Pallas kernels: 0 us -> 26.9 us
  starting transfers between devices: 17.9 us -> 0.01 us
  matrix products: 15.7 us -> 0 us
  between operations: 13.6 us -> 24.9 us
  local copies, waits for them, and re-layouts: 2.54 us -> 4.97 us
  other arithmetic: 6.77 us -> 8.86 us
    all_gather x1, waiting for transfers between devices: 76.8 us -> 39.7 us  [local(): pool = lax.all_gather(jnp.concatenate(sent), 'dom', axis=0, tiled=True)]
    ppermute x16 -> x0, waiting for transfers between devices: 31.9 us -> none  [the longest x8 17.2 us: extended(): lax.ppermute(tail, axis, [(i, (i + 1) % count) for i in range(count)])]
    pallas_call x0 -> x1, Pallas kernels: none -> 26.9 us  [advance(): pl.pallas_call(functools.partial(advance_kernel, count, groups), out_shap...]
    ppermute x16 -> x0, starting transfers between devices: 17.9 us -> none  [the longest x8 14 us: extended(): lax.ppermute(tail, axis, [(i, (i + 1) % count) for i in range(count)])]
    dot_general x1 -> x0, matrix products: 15.7 us -> none  [local(): jnp.einsum('jk,kfrc->jfrc', select, piece, precision=lax.Precision.HIGHEST)]
    select_n x0 -> x2, other arithmetic: none -> 4.01 us  [the longest x1 4 us: local(): copied.append(jnp.where(moved[j], got, state[k:k + 1]))]
    mul x4 -> x0, other arithmetic: 3.08 us -> none  [local(): depth * across]
    unnamed x10 -> x11, local copies, waits for them, and re-layouts: 0.02 us -> 2.46 us
  transfers between devices with their start and end apart: 17 -> 1, of which waited for: 17 -> 1; matrix products, arithmetic and copies ran while one was open for 0% -> 1% of each run, Pallas kernels for 0% -> 0%
where the time goes in v1:
time: 106 us; the launch traced here: 105 us
  waiting for transfers between devices  39.7 us (37%)
  Pallas kernels  26.9 us (25%)
  between operations  24.9 us (23%)
  other arithmetic  8.86 us (8%)
  local copies, waits for them, and re-layouts  4.97 us (5%)
    all_gather x1, waiting for transfers between devices, local(): pool = lax.all_gather(jnp.concatenate(sent), 'dom', axis=0, tiled=True)  39.7 us
    pallas_call x1, Pallas kernels, advance(): pl.pallas_call(functools.partial(advance_kernel, count, groups), out_shap...  26.9 us
    select_n x1, other arithmetic, local(): copied.append(jnp.where(moved[j], got, state[k:k + 1]))  4 us
    unnamed x11, local copies, waits for them, and re-layouts  2.46 us
  transfers between devices with their start and end apart: 1, of which 1 were waited for; matrix products, arithmetic and copies ran while one was open for 1% of the time, Pallas kernels for 0%

profile of v1, /device:TPU:0, one launch (start us, length us, event | category | flops | bytes accessed | tf_op | source)
XLA Modules:
  0.0 105.4 jit_solution(14660286409611586618)
XLA Ops:
  6.5 0.0 all-gather.2.cloned.1.call-start
  6.5 0.7 iota_compare_fusion.2
  7.2 0.7 fusion.1
  7.9 0.2 convert_reduce_fusion
  8.1 0.8 select_reduce_fusion
  9.0 1.4 %fusion.4 = (s32[]{:T(128)}, s32[]{:T(128)}, s32[32]{0:T(128)S(1)}) fusion(pred[32]{0:T(512)(128)(4,1)S(1)} %fusion.1, s32[32]{0:T(128)S(1)} %convert_reduce_fusion, s32[]{:T(128)S(6)} %mul.7, s32[]{:T(128)S(6)} %select_n.107, s32[32]{0:T(128)S(1)} %select_reduce_fusion, s32[32]{0:T(128)} %param.6), kind=kLoop, calls=%fused_computation.29 | loop fusion | flops 1182 | bytes 560 | tf_op jit(solution)/shard_map/reduce_sum | solution.py:216
  14.4 1.2 %constant_dynamic-slice_fusion.1 = (f32[1,3,16,2048]{3,2,1,0:T(8,128)S(1)}, f32[1,3,16,2048]{3,2,1,0:T(8,128)S(1)}) fusion(f32[4,3,16,2048]{3,2,1,0:T(8,128)} %param.7, s32[]{:T(128)S(6)} %select_n.109, s32[]{:T(128)S(6)} %select_n.111), kind=kLoop, calls=%fused_computation.19 | loop fusion | bytes 1572872 | tf_op jit(solution)/shard_map/dynamic_slice | solution.py:217
  15.6 0.0 copy-start.4
  15.6 0.9 pad_maximum_fusion.1
  16.5 0.0 all-gather.2.cloned.1.call-update
  16.5 0.7 fusion.7
  24.6 0.7 fusion.6
  25.3 39.7 %all-gather.2.cloned.1.call-done = f32[16,3,16,2048]{3,2,1,0:T(8,128)} async-done(((f32[2,3,16,2048]{3,2,1,0:T(8,128)}), f32[16,3,16,2048]{3,2,1,0:T(8,128)}) %all-gather.2.cloned.1.call-update) | async-done | bytes 6291472 | tf_op jit(solution)/shard_map/all_gather | solution.py:218
  65.0 0.0 copy-done.4
  65.0 4.0 %slice_select_fusion.3 = (f32[1,3,16,2048]{3,2,1,0:T(8,128)S(1)}, f32[1,3,16,2048]{3,2,1,0:T(8,128)S(1)}, f32[1,3,16,2048]{3,2,1,0:T(8,128)S(1)}, f32[1,3,16,2048]{3,2,1,0:T(8,128)S(1)}) fusion(f32[4,3,16,2048]{3,2,1,0:T(8,128)S(1)} %copy-done.4, f32[16,3,16,2048]{3,2,1,0:T(8,128)} %all-gather.2.cloned.1.call-done, s32[]{:T(128)S(6)} %select_n.114, ...), kind=kLoop, calls=%fused_computation.5 | loop fusion | flops 393216 | bytes 4718612 | tf_op jit(solution)/shard_map/jit(_where)/select_n | solution.py:226
  69.0 0.0 copy-start
  69.0 0.0 copy-start.1
  69.0 0.0 copy-start.2
  69.0 0.0 copy-start.3
  69.0 0.1 pad_maximum_fusion.copied
  69.1 1.3 %copy-done = f32[4,3,16,2048]{3,2,1,0:T(8,128)S(1)} copy-done((f32[4,3,16,2048]{3,2,1,0:T(8,128)S(1)}, f32[4,3,16,2048]{3,2,1,0:T(8,128)}, u32[]{:S(2)}) %copy-start) | copy-done | bytes 1572888
  70.4 0.0 copy-done.1
  70.4 0.0 copy-done.2
  70.4 0.0 copy-done.3
  70.4 26.9 %advance.1 = f32[4,3,16,2048]{3,2,1,0:T(8,128)S(1)} custom-call(f32[4,3,16,2048]{3,2,1,0:T(8,128)S(1)} %pad_maximum_fusion.copied, f32[4,3,16,2048]{3,2,1,0:T(8,128)S(1)} %copy-done, f32[16,2048]{1,0:T(8,128)S(1)} %copy-done.1, f32[16,2048]{1,0:T(8,128)S(1)} %copy-done.2, f32[16,2048]{1,0:T(8,128)S(1)} %copy-done.3), custom_call_target="tpu_custom_call" | custom-call | tf_op jit(solution)/shard_map/advance/pallas_call | solution.py:180
  97.4 1.1 %copy.8 = f32[4,3,16,2048]{3,2,1,0:T(8,128)} copy(f32[4,3,16,2048]{3,2,1,0:T(8,128)S(1)} %advance.1) | data formatting | bytes 3145728
  (1 shorter events, 0.0 us)
Async XLA Ops:
  6.5 58.4 %all-gather.2.cloned.1.call-start = ((), (), s32[]{:S(2)}) async-start(), calls=%async_computation | async-start | bytes 7077888 | tf_op jit(solution)/shard_map/all_gather | solution.py:218
  15.6 49.4 %copy-start.4 = (f32[4,3,16,2048]{3,2,1,0:T(8,128)S(1)}, f32[4,3,16,2048]{3,2,1,0:T(8,128)}, u32[]{:S(2)}) copy-start(f32[4,3,16,2048]{3,2,1,0:T(8,128)} %param.7) | copy-start | bytes 4718596
  69.0 1.4 %copy-start = (f32[4,3,16,2048]{3,2,1,0:T(8,128)S(1)}, f32[4,3,16,2048]{3,2,1,0:T(8,128)}, u32[]{:S(2)}) copy-start(f32[4,3,16,2048]{3,2,1,0:T(8,128)} %jitter.1) | copy-start | bytes 4718596
  69.0 1.4 %copy-start.1 = (f32[16,2048]{1,0:T(8,128)S(1)}, f32[16,2048]{1,0:T(8,128)}, u32[]{:S(2)}) copy-start(f32[16,2048]{1,0:T(8,128)} %depth.1) | copy-start | bytes 393220
  69.0 1.4 %copy-start.2 = (f32[16,2048]{1,0:T(8,128)S(1)}, f32[16,2048]{1,0:T(8,128)}, u32[]{:S(2)}) copy-start(f32[16,2048]{1,0:T(8,128)} %coriolis.1) | copy-start | bytes 393220
  69.0 1.4 %copy-start.3 = (f32[16,2048]{1,0:T(8,128)S(1)}, f32[16,2048]{1,0:T(8,128)}, u32[]{:S(2)}) copy-start(f32[16,2048]{1,0:T(8,128)} %drag.1) | copy-start | bytes 393220
Sparse Core Ops, SparseCore 0:
  16.7 48.2 all-gather.1

commit v2 on v1

--- a/solution.py
+++ b/solution.py
@@ -33,7 +33,7 @@
 
 def advance_kernel(
     count, groups,
-    copied, jitter, depth, coriolis, drag, out,
+    fields, depth, coriolis, drag, out,
     flux_c, keep_c, turn_c, push_c, rim_send, rim_recv, send, recv, last_send, last_recv, halo,
     send_sem, recv_sem,
 ):
@@ -70,9 +70,9 @@
             for i in range(each):
                 p = group * each + i
                 for k, part in enumerate((1, 2)):
-                    send[0, group, side, k * each + i : k * each + i + 1, :] = (
-                        copied[p, part, row : row + 1, :] + jitter[p, part, row : row + 1, :]
-                    )
+                    send[0, group, side, k * each + i : k * each + i + 1, :] = fields[
+                        p, part, row : row + 1, :
+                    ]
     pl.semaphore_wait(barrier, 2)
     for side in (UP, DOWN):
         rim(side).start()
@@ -86,7 +86,7 @@
     turn_c[...] = DT * coriolis[...] * keep
     push_c[...] = 0.5 * DT * keep
     for p in range(members):
-        out[p] = copied[p] + jitter[p]
+        out[p] = fields[p]
     for side in (UP, DOWN):
         rim(side).wait_recv()
     edge = []
@@ -170,8 +170,8 @@
                 swap(step, group, side).wait_send()
 
 
-def advance(copied, jitter, depth, coriolis, drag, count):
-    members, _, rows, width = jitter.shape
+def advance(fields, depth, coriolis, drag, count):
+    members, _, rows, width = fields.shape
     groups = 2
     each = members // groups
     f32 = jnp.float32
@@ -179,8 +179,8 @@
     copies = 1 + (STEPS + 1) * groups
     return pl.pallas_call(
         functools.partial(advance_kernel, count, groups),
-        out_shape=jax.ShapeDtypeStruct(jitter.shape, f32),
-        in_specs=[pl.BlockSpec(memory_space=pltpu.VMEM)] * 5,
+        out_shape=jax.ShapeDtypeStruct(fields.shape, f32),
+        in_specs=[pl.BlockSpec(memory_space=pltpu.VMEM)] * 4,
         out_specs=pl.BlockSpec(memory_space=pltpu.VMEM),
         scratch_shapes=[
             plane, plane, plane, plane,
@@ -198,10 +198,202 @@
             collective_id=0, has_side_effects=True, vmem_limit_bytes=40 * 1024 * 1024
         ),
         name="advance",
-    )(copied, jitter, depth, coriolis, drag)
-
-
-def local(count, ancestor, state, jitter, depth, coriolis, drag):
+    )(fields, depth, coriolis, drag)
+
+
+def routes_kernel(members, across, down, out):
+    part = across.shape[1]
+    me = lax.axis_index("dom")
+    chip = me // 2
+    lane = lax.broadcasted_iota(jnp.int32, (part, part), 1)
+    sub = lax.broadcasted_iota(jnp.int32, (part, part), 0)
+    row_p, col_p = lane[0:1, :], sub[:, 0:1]
+
+    def over(mask, value, axis):
+        return jnp.sum(jnp.where(mask, value, 0), axis=axis, keepdims=True)
+
+    target_row = over((down[...] == lane) & (sub != lane), sub + 1, 0) - 1
+    target_col = over((across[...] == sub) & (sub != lane), lane + 1, 1) - 1
+
+    def chip_of(p):
+        return lax.shift_right_arithmetic(p, (2 * members).bit_length() - 1)
+
+    def block_of(p):
+        return lax.shift_right_arithmetic(p, members.bit_length() - 1)
+
+    d_row = jnp.where(target_row >= 0, chip_of(row_p) ^ chip_of(target_row), 0)
+    d_col = jnp.where(target_col >= 0, chip_of(col_p) ^ chip_of(target_col), 0)
+    rank = over((target_col >= 0) & (sub < lane) & (block_of(sub) == block_of(lane)), 1, 0)
+    own = (block_of(row_p) & 1) * CAP + rank
+
+    columns = [None] * 8
+    most_first, most_second = jnp.int32(0), jnp.int32(0)
+    for q in range(2):
+        first, second = 1 + q, 2 - q
+        f_row, f_col = (d_row & first) != 0, (d_col & first) != 0
+        g_row, g_col = (d_row & second) != 0, (d_col & second) != 0
+        s1 = over(f_col & (chip_of(sub) == chip_of(lane)) & (sub < lane), 1, 0)
+        e_row = chip_of(row_p) ^ (d_row & first)
+        e_col = chip_of(col_p) ^ (d_col & first)
+        key_row = row_p + jnp.where(f_row, part, 0)
+        key_col = col_p + jnp.where(f_col, part, 0)
+        s2 = over(g_col & (e_col == e_row) & (key_col < key_row), 1, 0)
+        found = jnp.where(g_row, 4 * CAP + s2, jnp.where(f_row, 2 * CAP + s1, own))
+        columns[q] = over((s1 == sub) & f_row & (chip_of(row_p) == chip), own, 1)
+        columns[2 + q] = over(
+            (s2 == sub) & g_row & (e_row == chip), jnp.where(f_row, 2 * CAP + s1, own), 1
+        )
+        columns[4 + q] = over(target_row == sub, found, 1)
+        most_first = jnp.maximum(most_first, jnp.max(jnp.where(f_row, s1 + 1, 0)))
+        most_second = jnp.maximum(most_second, jnp.max(jnp.where(g_row, s2 + 1, 0)))
+    columns[6] = jnp.where(down[...] != col_p, 1, 0)
+    tier = jnp.int32(len(TIERS))
+    for n in range(len(TIERS) - 1, -1, -1):
+        fits = (most_first <= TIERS[n][0]) & (most_second <= TIERS[n][1])
+        tier = jnp.where(fits, n, tier)
+    mine = over((rank == sub) & (target_row >= 0) & (block_of(row_p) == me), row_p & (members - 1), 1)
+    columns[7] = jnp.where(col_p < CAP, mine, tier)
+    for k in range(8):
+        out[:, k : k + 1] = columns[k]
+
+
+TIERS = ((2, 2), (3, 3))
+
+
+def resample_kernel(
+    c1, c2,
+    table, state, jitter, out,
+    own0, own1, first_send0, first_send1, first_recv0, first_recv1,
+    second_send0, second_send1, second_recv0, second_recv1, core_send, last_send, last_recv,
+    send_sem, recv_sem,
+):
+    members, _, rows, width = out.shape
+    half, wide = rows // 2, width // 2
+    me = lax.axis_index("dom")
+    core = lax.rem(me, 2)
+    chip = me // 2
+    other = me + 1 - 2 * core
+    turned = (me + 2 - 4 * lax.rem(chip, 2), me + 4 - 8 * (chip // 2))
+    own, first_send, first_recv = (own0, own1), (first_send0, first_send1), (first_recv0, first_recv1)
+    second_send, second_recv = (second_send0, second_send1), (second_recv0, second_recv1)
+    mine, theirs = pl.multiple_of(core * half, half), pl.multiple_of((1 - core) * half, half)
+
+    barrier = pltpu.get_barrier_semaphore()
+    for device in (other,) + turned:
+        pl.semaphore_signal(barrier, inc=1, device_id={"dom": device}, device_id_type=MESH)
+
+    def send(number, source, target, device):
+        return pltpu.make_async_remote_copy(
+            src_ref=source, dst_ref=target, send_sem=send_sem.at[number], recv_sem=recv_sem.at[number],
+            device_id={"dom": device}, device_id_type=MESH,
+        )
+
+    cores = [
+        send(q, core_send.at[q], own[q].at[pl.ds(core * CAP, CAP)], other) for q in range(2)
+    ]
+    firsts = [send(2 + q, first_send[q], first_recv[q], turned[q]) for q in range(2)]
+    seconds = [send(4 + q, second_send[q], second_recv[q], turned[1 - q]) for q in range(2)]
+    last = send(6, last_send, last_recv, other)
+
+    for k in range(CAP):
+        slot = table[k, 7]
+        for q in range(2):
+            columns = pl.ds(q * wide, wide)
+            core_send[q, k] = state[slot, :, pl.ds(theirs, half), columns]
+            own[q][core * CAP + k] = state[slot, :, pl.ds(mine, half), columns]
+    pl.semaphore_wait(barrier, 3)
+    for copy in cores:
+        copy.start()
+    for copy in cores:
+        copy.wait_recv()
+    for q in range(2):
+        for k in range(c1):
+            first_send[q][k] = own[q][table[k, q]]
+        firsts[q].start()
+
+    def pick(q, index, come):
+        value = own[q][jnp.clip(index, 0, 2 * CAP - 1)]
+        value = jnp.where(index >= 2 * CAP, first_recv[q][jnp.clip(index - 2 * CAP, 0, c1 - 1)], value)
+        if come:
+            value = jnp.where(
+                index >= 4 * CAP, second_recv[q][jnp.clip(index - 4 * CAP, 0, c2 - 1)], value
+            )
+        return value
+
+    for q in range(2):
+        firsts[q].wait_recv()
+        for k in range(c2):
+            second_send[q][k] = pick(q, table[k, 2 + q], False)
+        seconds[q].start()
+    for q in range(2):
+        seconds[q].wait_recv()
+    for k in range(members):
+        for q in range(2):
+            last_send[k, :, :, q * wide : (q + 1) * wide] = pick(q, table[other * members + k, 4 + q], True)
+    last.start()
+    for k in range(members):
+        moved = table[me * members + k, 6]
+        for q in range(2):
+            columns = pl.ds(q * wide, wide)
+            got = pick(q, table[me * members + k, 4 + q], True)
+            kept = state[k, :, pl.ds(mine, half), columns]
+            out[k, :, pl.ds(mine, half), columns] = (
+                jnp.where(moved != 0, got, kept) + jitter[k, :, pl.ds(mine, half), columns]
+            )
+    last.wait_recv()
+    for k in range(members):
+        moved = table[me * members + k, 6]
+        kept = state[k, :, pl.ds(theirs, half), :]
+        out[k, :, pl.ds(theirs, half), :] = (
+            jnp.where(moved != 0, last_recv[k], kept) + jitter[k, :, pl.ds(theirs, half), :]
+        )
+    for copy in cores + firsts + seconds + [last]:
+        copy.wait_send()
+
+
+def resample(number, c1, c2, table, state, jitter):
+    members, parts, rows, width = state.shape
+    f32 = jnp.float32
+
+    def slots(n, wide=width // 2):
+        return pltpu.VMEM((n, parts, rows // 2, wide), f32)
+
+    return pl.pallas_call(
+        functools.partial(resample_kernel, c1, c2),
+        out_shape=jax.ShapeDtypeStruct(state.shape, f32),
+        in_specs=[pl.BlockSpec(memory_space=pltpu.SMEM)] + [pl.BlockSpec(memory_space=pltpu.VMEM)] * 2,
+        out_specs=pl.BlockSpec(memory_space=pltpu.VMEM),
+        scratch_shapes=[slots(2 * CAP)] * 2
+        + [slots(c1)] * 4
+        + [slots(c2)] * 4
+        + [pltpu.VMEM((2, CAP, parts, rows // 2, width // 2), f32), slots(members, width), slots(members, width)]
+        + [pltpu.SemaphoreType.DMA((7,))] * 2,
+        compiler_params=pltpu.CompilerParams(
+            collective_id=number, has_side_effects=True, vmem_limit_bytes=40 * 1024 * 1024
+        ),
+        name="resample",
+    )(table, state, jitter)
+
+
+def routed(ancestor, state, jitter):
+    members = state.shape[0]
+    part = ancestor.shape[0]
+    table = pl.pallas_call(
+        functools.partial(routes_kernel, members),
+        out_shape=jax.ShapeDtypeStruct((part, 8), jnp.int32),
+        in_specs=[pl.BlockSpec(memory_space=pltpu.VMEM)] * 2,
+        out_specs=pl.BlockSpec(memory_space=pltpu.VMEM),
+        name="routes",
+    )(ancestor[None, :], ancestor[:, None])
+    sizes = TIERS + ((2 * CAP, 2 * members),)
+    return lax.switch(
+        table[CAP, 7],
+        [functools.partial(resample, 1 + n, c1, c2) for n, (c1, c2) in enumerate(sizes)],
+        table, state, jitter,
+    )
+
+
+def gathered(ancestor, state, jitter):
     members = state.shape[0]
     part = ancestor.shape[0]
     first = lax.axis_index("dom") * members
@@ -224,14 +416,21 @@
         j = first + k
         got = lax.dynamic_slice_in_dim(pool, where[j], 1)
         copied.append(jnp.where(moved[j], got, state[k : k + 1]))
-    return advance(jnp.concatenate(copied), jitter, depth, coriolis, drag, count)
+    return jnp.concatenate(copied) + jitter
+
+
+def local(count, doms, ancestor, state, jitter, depth, coriolis, drag):
+    members = state.shape[0]
+    simple = doms == 8 and members == 4 and state.shape[2] % 16 == 0
+    fields = (routed if simple else gathered)(ancestor, state, jitter)
+    return advance(fields, depth, coriolis, drag, count)
 
 
 def solution(mesh):
     field = P("dom", None, "space", None)
     plane = P("space", None)
     return jax.shard_map(
-        functools.partial(local, mesh.shape["space"]),
+        functools.partial(local, mesh.shape["space"], mesh.shape["dom"]),
         mesh=mesh,
         in_specs=(P(), field, field, plane, plane, plane),
         out_specs=field,

time: 106 us -> 57.8 us (0.55)
  waiting for transfers between devices: 39.7 us -> 0 us
  Pallas kernels: 26.9 us -> 53.7 us
  between operations: 24.9 us -> 0.73 us
  other arithmetic: 8.86 us -> 0 us
  local copies, waits for them, and re-layouts: 4.97 us -> 3.09 us
    all_gather x1 -> x0, waiting for transfers between devices: 39.7 us -> none  [local(): pool = lax.all_gather(jnp.concatenate(sent), 'dom', axis=0, tiled=True)]
    pallas_call x0 -> x2, Pallas kernels: none -> 26.3 us  [the longest x1 25.3 us: resample(): pl.pallas_call(functools.partial(resample_kernel, c1, c2), out_shape=jax....]
    select_n x2 -> x0, other arithmetic: 4.01 us -> none  [the longest x1 4 us: local(): copied.append(jnp.where(moved[j], got, state[k:k + 1]))]
    dynamic_slice x3 -> x0, local copies, waits for them, and re-layouts: 2.51 us -> none  [the longest x1 1.17 us: local(): sent.append(lax.dynamic_slice_in_dim(state, slot, 1))]
    reduce_sum x3 -> x0, other arithmetic: 2.41 us -> none  [the longest x1 1.38 us: local(): slot = jnp.sum(jnp.where(hit, index - first, 0))]
    broadcast_in_dim x0 -> x1, local copies, waits for them, and re-layouts: none -> 1.34 us  [routed(): ancestor[:, None]]
    unnamed x11 -> x7, local copies, waits for them, and re-layouts: 2.46 us -> 1.16 us
  transfers between devices with their start and end apart: 1 -> 0, of which waited for: 1 -> 0; matrix products, arithmetic and copies ran while one was open for 1% -> 0% of each run, Pallas kernels for 0% -> 0%
where the time goes in v2:
time: 57.8 us; the launch traced here: 57.6 us
  Pallas kernels  53.7 us (93%)
  local copies, waits for them, and re-layouts  3.09 us (5%)
  between operations  0.73 us (1%)
    pallas_call x1, Pallas kernels, advance(): pl.pallas_call(functools.partial(advance_kernel, count, groups), out_shap...  27.4 us
    pallas_call x1, Pallas kernels, resample(): pl.pallas_call(functools.partial(resample_kernel, c1, c2), out_shape=jax....  25.3 us
    broadcast_in_dim x1, local copies, waits for them, and re-layouts, routed(): ancestor[:, None]  1.34 us
    unnamed x7, local copies, waits for them, and re-layouts  1.16 us

profile of v2, /device:TPU:0, one launch (start us, length us, event | category | flops | bytes accessed | tf_op | source)
XLA Modules:
  0.0 57.6 jit_solution(3932933769426906308)
XLA Ops:
  0.0 1.3 %copy.7.down = s32[32,1]{1,0:T(8,128)} copy(s32[32,1]{0,1:T(1,128)} %bitcast.3) | data formatting | bytes 256 | tf_op jit(solution)/shard_map/broadcast_in_dim | solution.py:387
  1.3 1.1 %routes.1 = s32[32,8]{1,0:T(8,128)S(1)} custom-call(s32[1,32]{1,0:T(1,128)} %bitcast.4, s32[32,1]{1,0:T(8,128)} %copy.7.down), custom_call_target="tpu_custom_call" | custom-call | tf_op jit(solution)/shard_map/routes/pallas_call | solution.py:381
  2.4 0.6 %slice.4 = s32[1,1]{1,0:T(1,128)} slice(s32[32,8]{1,0:T(8,128)S(1)} %routes.1), slice={[2:3], [7:8]} | slice | bytes 8 | tf_op jit(solution)/shard_map/slice | solution.py:390
  3.6 0.0 copy-start
  3.7 0.0 copy-start.1
  3.7 0.0 copy-start.2
  3.7 25.3 %conditional.1 = (f32[4,3,16,2048]{3,2,1,0:T(8,128)S(1)}) conditional(s32[]{:T(128)} %bitcast.2, (s32[32,8]{1,0:T(8,128)S(1)}, f32[4,3,16,2048]{3,2,1,0:T(8,128)}, f32[4,3,16,2048]{3,2,1,0:T(8,128)}) %tuple.14, (s32[32,8]{1,0:T(8,128)S(1)}, f32[4,3,16,2048]{3,2,1,0:T(8,128)}, f32[4,3,16,2048]{3,2,1,0:T(8,128)}) %tuple.14, ...), branch_computations={%region_0.0_spmd, %region_1.0_spmd, %region_2.0_spmd} | conditional | bytes 8 | solution.py:389
  3.7 25.3 %resample.4 = f32[4,3,16,2048]{3,2,1,0:T(8,128)S(1)} custom-call(s32[32,8]{1,0:T(8,128)S(1)} %get-tuple-element.30.table, f32[4,3,16,2048]{3,2,1,0:T(8,128)} %get-tuple-element.31.state, f32[4,3,16,2048]{3,2,1,0:T(8,128)} %get-tuple-element.32.jitter), custom_call_target="tpu_custom_call" | custom-call | tf_op jit(solution)/shard_map/cond/branch_1_fun/resample/pallas_call | solution.py:361
  29.0 0.0 copy-done
  29.0 0.0 copy-done.1
  29.0 0.0 copy-done.2
  29.0 27.4 %advance.1 = f32[4,3,16,2048]{3,2,1,0:T(8,128)S(1)} custom-call(f32[4,3,16,2048]{3,2,1,0:T(8,128)S(1)} %get-tuple-element.36.fields, f32[16,2048]{1,0:T(8,128)S(1)} %copy-done, f32[16,2048]{1,0:T(8,128)S(1)} %copy-done.1, f32[16,2048]{1,0:T(8,128)S(1)} %copy-done.2), custom_call_target="tpu_custom_call" | custom-call | tf_op jit(solution)/shard_map/advance/pallas_call | solution.py:180
  56.4 1.1 %copy.12 = f32[4,3,16,2048]{3,2,1,0:T(8,128)} copy(f32[4,3,16,2048]{3,2,1,0:T(8,128)S(1)} %advance.1) | data formatting | bytes 3145728
Async XLA Ops:
  3.6 25.4 %copy-start = (f32[16,2048]{1,0:T(8,128)S(1)}, f32[16,2048]{1,0:T(8,128)}, u32[]{:S(2)}) copy-start(f32[16,2048]{1,0:T(8,128)} %depth.1) | copy-start | bytes 393220
  3.7 25.4 %copy-start.1 = (f32[16,2048]{1,0:T(8,128)S(1)}, f32[16,2048]{1,0:T(8,128)}, u32[]{:S(2)}) copy-start(f32[16,2048]{1,0:T(8,128)} %coriolis.1) | copy-start | bytes 393220
  3.7 25.4 %copy-start.2 = (f32[16,2048]{1,0:T(8,128)S(1)}, f32[16,2048]{1,0:T(8,128)}, u32[]{:S(2)}) copy-start(f32[16,2048]{1,0:T(8,128)} %drag.1) | copy-start | bytes 393220

commit v3 on v2

v3 whole, which is shorter than its diff:
```python
import functools

import jax
import jax.numpy as jnp
from jax import lax
from jax.experimental import pallas as pl
from jax.experimental.pallas import tpu as pltpu
from jax.sharding import PartitionSpec as P

STEPS = 4
DT = 0.3
CAP = 2
MESH = pl.DeviceIdType.MESH
UP, DOWN = 0, 1


def column_difference(a, edge):
    width = a.shape[1]
    column = lax.broadcasted_iota(jnp.int32, a.shape, 1)
    beyond = a if edge else jnp.zeros_like(a)
    after = jnp.where(column == width - 1, beyond, pltpu.roll(a, width - 1, 1))
    before = jnp.where(column == 0, beyond, pltpu.roll(a, 1, 1))
    return after - before


def row_difference(a, above, below):
    rows = a.shape[0]
    row = lax.broadcasted_iota(jnp.int32, a.shape, 0)
    after = jnp.where(row == rows - 1, below, pltpu.roll(a, rows - 1, 0))
    before = jnp.where(row == 0, above, pltpu.roll(a, 1, 0))
    return after - before


def exchange(axis, number, source, target, device, send_sem, recv_sem):
    return pltpu.make_async_remote_copy(
        src_ref=source, dst_ref=target, send_sem=send_sem.at[number], recv_sem=recv_sem.at[number],
        device_id={axis: device}, device_id_type=MESH,
    )


def advance_kernel(
    count, groups,
    fields, depth, coriolis, drag, rim, out,
    flux_c, keep_c, turn_c, push_c, rim_c, send, recv, last_send, last_recv, halo, near, far,
    send_sem, recv_sem,
):
    members, _, rows, width = out.shape
    each = members // groups
    me = lax.axis_index("space")
    towards = (lax.rem(me + count - 1, count), lax.rem(me + 1, count))

    barrier = pltpu.get_barrier_semaphore()
    for neighbour in towards:
        pl.semaphore_signal(barrier, inc=1, device_id={"space": neighbour}, device_id_type=MESH)

    def swap(step, group, side):
        number = 2 * (step * groups + group) + side
        if step == STEPS:
            source, target = last_send.at[group, side], last_recv.at[group, 1 - side]
        else:
            source, target = send.at[step, group, side], recv.at[step, group, 1 - side]
        return exchange("space", number, source, target, towards[side], send_sem, recv_sem)

    for group in range(groups):
        for side, row in ((UP, 0), (DOWN, rows - 1)):
            for i in range(each):
                for k in range(2):
                    at = slice(k * each + i, k * each + i + 1)
                    send[0, group, side, at, :] = fields[group * each + i, 1 + k, row : row + 1, :]
    pl.semaphore_wait(barrier, 2)
    for group in range(groups):
        for side in (UP, DOWN):
            swap(0, group, side).start()

    keep = 1.0 / (1.0 + DT * drag[...])
    flux_c[...] = 0.5 * DT * depth[...]
    keep_c[...] = keep
    turn_c[...] = DT * coriolis[...] * keep
    push_c[...] = 0.5 * DT * keep
    for side in (UP, DOWN):
        rim_depth, rim_coriolis, rim_drag = (rim[side, k : k + 1, :] for k in range(3))
        k = 1.0 / (1.0 + DT * rim_drag)
        for i in range(each):
            at = slice(side * each + i, side * each + i + 1)
            rim_c[0, at, :] = 0.5 * DT * rim_depth
            rim_c[1, at, :] = k
            rim_c[2, at, :] = DT * rim_coriolis * k
            rim_c[3, at, :] = 0.5 * DT * k
            rim_c[4, at, :] = 0.5 * DT * k if side == UP else -0.5 * DT * k

    def finish(step, group):
        for side in (UP, DOWN):
            swap(step, group, side).wait_recv()
        come = last_recv.at[group] if step == STEPS else recv.at[step, group]
        if step < STEPS:
            for side in (UP, DOWN):
                at = slice(side * each, (side + 1) * each)
                near[at, :] = come[side, 0:each, :]
                far[at, :] = send[step, group, side, 0:each, :] - come[side, each : 2 * each, :]
            u, v = halo[group, 0], halo[group, 1]
            halo[group, 0] = u * rim_c[1] + v * rim_c[2] - rim_c[3] * column_difference(near[...], True)
            halo[group, 1] = v * rim_c[1] - u * rim_c[2] - rim_c[4] * far[...]
        for i in range(each):
            p = group * each + i
            out[p, 2] = out[p, 2] - push_c[...] * row_difference(
                out[p, 0], come[UP, i : i + 1, :], come[DOWN, i : i + 1, :]
            )

    for step in range(1, STEPS + 1):
        old = fields if step == 1 else out
        for group in range(groups):
            if step == 1:
                for side in (UP, DOWN):
                    swap(0, group, side).wait_recv()
                for side in (UP, DOWN):
                    for k in range(2):
                        halo[group, k, side * each : (side + 1) * each, :] = recv[
                            0, group, side, k * each : (k + 1) * each, :
                        ]
            else:
                finish(step - 1, group)
            near[...] = rim_c[0] * halo[group, 1]
            for i in range(each):
                p = group * each + i
                f = flux_c[...]
                height = old[p, 0] - (
                    column_difference(f * old[p, 1], False)
                    + row_difference(f * old[p, 2], near[i : i + 1, :], near[each + i : each + i + 1, :])
                )
                out[p, 0] = height
                if step == STEPS:
                    last_send[group, UP, i : i + 1, :] = height[0:1, :]
                    last_send[group, DOWN, i : i + 1, :] = height[rows - 1 : rows, :]
                else:
                    for k in range(2):
                        at = slice(k * each + i, k * each + i + 1)
                        send[step, group, UP, at, :] = height[k : k + 1, :]
                        send[step, group, DOWN, at, :] = height[rows - 1 - k : rows - k, :]
            for side in (UP, DOWN):
                swap(step, group, side).start()
            for i in range(each):
                p = group * each + i
                u, v = old[p, 1], old[p, 2]
                out[p, 1] = u * keep_c[...] + turn_c[...] * v - push_c[...] * column_difference(out[p, 0], True)
                out[p, 2] = v * keep_c[...] - turn_c[...] * u
    for group in range(groups):
        finish(STEPS, group)
    for step in range(STEPS + 1):
        for group in range(groups):
            for side in (UP, DOWN):
                swap(step, group, side).wait_send()


def advance(fields, depth, coriolis, drag, rim, count):
    members, _, rows, width = fields.shape
    groups = 2
    each = members // groups
    f32 = jnp.float32
    plane = pltpu.VMEM((rows, width), f32)
    edges = pltpu.VMEM((2 * each, width), f32)
    copies = 2 * (STEPS + 1) * groups
    return pl.pallas_call(
        functools.partial(advance_kernel, count, groups),
        out_shape=jax.ShapeDtypeStruct(fields.shape, f32),
        in_specs=[pl.BlockSpec(memory_space=pltpu.VMEM)] * 5,
        out_specs=pl.BlockSpec(memory_space=pltpu.VMEM),
        scratch_shapes=[
            plane, plane, plane, plane,
            pltpu.VMEM((5, 2 * each, width), f32),
            pltpu.VMEM((STEPS, groups, 2, 2 * each, width), f32),
            pltpu.VMEM((STEPS, groups, 2, 2 * each, width), f32),
            pltpu.VMEM((groups, 2, each, width), f32),
            pltpu.VMEM((groups, 2, each, width), f32),
            pltpu.VMEM((groups, 2, 2 * each, width), f32),
            edges, edges,
            pltpu.SemaphoreType.DMA((copies,)),
            pltpu.SemaphoreType.DMA((copies,)),
        ],
        compiler_params=pltpu.CompilerParams(
            collective_id=0, has_side_effects=True, vmem_limit_bytes=40 * 1024 * 1024
        ),
        name="advance",
    )(fields, depth, coriolis, drag, rim)


def routes_kernel(members, across, out, tier_out):
    part = across.shape[1]
    me = lax.axis_index("dom")
    chip = me // 2
    lane = lax.broadcasted_iota(jnp.int32, (part, part), 1)
    sub = lax.broadcasted_iota(jnp.int32, (part, part), 0)
    row_p, col_p = lane[0:1, :], sub[:, 0:1]
    down = jnp.sum(jnp.where(lane == sub, across[...], 0), axis=1, keepdims=True)

    def over(mask, value, axis):
        return jnp.sum(jnp.where(mask, value, 0), axis=axis, keepdims=True)

    target_row = over((down == lane) & (sub != lane), sub + 1, 0) - 1
    target_col = over((across[...] == sub) & (sub != lane), lane + 1, 1) - 1

    def chip_of(p):
        return lax.shift_right_arithmetic(p, (2 * members).bit_length() - 1)

    def block_of(p):
        return lax.shift_right_arithmetic(p, members.bit_length() - 1)

    d_row = jnp.where(target_row >= 0, chip_of(row_p) ^ chip_of(target_row), 0)
    d_col = jnp.where(target_col >= 0, chip_of(col_p) ^ chip_of(target_col), 0)
    rank = over((target_col >= 0) & (sub < lane) & (block_of(sub) == block_of(lane)), 1, 0)
    own = (block_of(row_p) & 1) * CAP + rank

    columns = [None] * 8
    most_first, most_second = jnp.int32(0), jnp.int32(0)
    for q in range(2):
        first, second = 1 + q, 2 - q
        f_row, f_col = (d_row & first) != 0, (d_col & first) != 0
        g_row, g_col = (d_row & second) != 0, (d_col & second) != 0
        s1 = over(f_col & (chip_of(sub) == chip_of(lane)) & (sub < lane), 1, 0)
        e_row = chip_of(row_p) ^ (d_row & first)
        e_col = chip_of(col_p) ^ (d_col & first)
        key_row = row_p + jnp.where(f_row, part, 0)
        key_col = col_p + jnp.where(f_col, part, 0)
        s2 = over(g_col & (e_col == e_row) & (key_col < key_row), 1, 0)
        found = jnp.where(g_row, 4 * CAP + s2, jnp.where(f_row, 2 * CAP + s1, own))
        columns[q] = over((s1 == sub) & f_row & (chip_of(row_p) == chip), own, 1)
        columns[2 + q] = over(
            (s2 == sub) & g_row & (e_row == chip), jnp.where(f_row, 2 * CAP + s1, own), 1
        )
        columns[4 + q] = over(target_row == sub, found, 1)
        most_first = jnp.maximum(most_first, jnp.max(jnp.where(f_row, s1 + 1, 0)))
        most_second = jnp.maximum(most_second, jnp.max(jnp.where(g_row, s2 + 1, 0)))
    columns[6] = jnp.where(down != col_p, 1, 0)
    tier = jnp.int32(len(TIERS))
    for n in range(len(TIERS) - 1, -1, -1):
        fits = (most_first <= TIERS[n][0]) & (most_second <= TIERS[n][1])
        tier = jnp.where(fits, n, tier)
    mine = over((rank == sub) & (target_row >= 0) & (block_of(row_p) == me), row_p & (members - 1), 1)
    columns[7] = mine
    tier_out[0] = tier
    for k in range(8):
        out[:, k : k + 1] = columns[k]


TIERS = ((2, 2), (3, 3), (4, 4))
PIECES = 4


def resample_kernel(
    c1, c2, count,
    table, state, jitter, depth, coriolis, drag, out, rim,
    rim_send, core_send, last_send, last_recv, own_all, first_send_all, first_recv_all, second_send_all, second_recv_all,
    send_sem, recv_sem, rim_send_sem, rim_recv_sem,
):
    members, _, rows, width = out.shape
    half, wide = rows // 2, width // PIECES
    pieces = range(PIECES)
    me = lax.axis_index("dom")
    core = lax.rem(me, 2)
    chip = me // 2
    other = me + 1 - 2 * core
    turned = (me + 2 - 4 * lax.rem(chip, 2), me + 4 - 8 * (chip // 2))
    slab = lax.axis_index("space")
    towards = (lax.rem(slab + count - 1, count), lax.rem(slab + 1, count))
    mine, theirs = pl.multiple_of(core * half, half), pl.multiple_of((1 - core) * half, half)

    barrier = pltpu.get_barrier_semaphore()
    for device in (other,) + turned:
        pl.semaphore_signal(barrier, inc=1, device_id={"dom": device}, device_id_type=MESH)
    for neighbour in towards:
        pl.semaphore_signal(barrier, inc=1, device_id={"space": neighbour}, device_id_type=MESH)

    def send(number, source, target, device):
        return exchange("dom", number, source, target, device, send_sem, recv_sem)

    rims = [
        exchange("space", side, rim_send.at[side], rim.at[1 - side], towards[side], rim_send_sem, rim_recv_sem)
        for side in (UP, DOWN)
    ]
    own, first_send, first_recv, second_send, second_recv = (
        tuple(ref for ref in refs) for refs in
        (own_all, first_send_all, first_recv_all, second_send_all, second_recv_all)
    )
    cores = [send(t, core_send.at[t], own[t].at[pl.ds(core * CAP, CAP)], other) for t in pieces]
    firsts = [send(PIECES + t, first_send[t], first_recv[t], turned[t % 2]) for t in pieces]
    seconds = [send(2 * PIECES + t, second_send[t], second_recv[t], turned[1 - t % 2]) for t in pieces]
    lasts = [send(3 * PIECES + t, last_send.at[t], last_recv.at[t], other) for t in pieces]

    for side, row in ((UP, 0), (DOWN, rows - 1)):
        for k, plane in enumerate((depth, coriolis, drag, drag)):
            rim_send[side, k : k + 1, :] = plane[row : row + 1, :]
    for t in pieces:
        columns = pl.ds(t * wide, wide)
        for k in range(CAP):
            slot = table[k, 7]
            core_send[t, k] = state[slot, :, pl.ds(theirs, half), columns]
            own[t][core * CAP + k] = state[slot, :, pl.ds(mine, half), columns]
    pl.semaphore_wait(barrier, 5)
    for t in pieces:
        cores[t].start()
    for copy in rims:
        copy.start()
    for t in pieces:
        cores[t].wait_recv()
        for k in range(c1):
            first_send[t][k] = own[t][table[k, t % 2]]
        firsts[t].start()

    def pick(t, index, come):
        value = own[t][jnp.clip(index, 0, 2 * CAP - 1)]
        value = jnp.where(index >= 2 * CAP, first_recv[t][jnp.clip(index - 2 * CAP, 0, c1 - 1)], value)
        if come:
            value = jnp.where(
                index >= 4 * CAP, second_recv[t][jnp.clip(index - 4 * CAP, 0, c2 - 1)], value
            )
        return value

    for t in pieces:
        firsts[t].wait_recv()
        for k in range(c2):
            second_send[t][k] = pick(t, table[k, 2 + t % 2], False)
        seconds[t].start()
    for t in pieces:
        seconds[t].wait_recv()
        for k in range(members):
            last_send[t, k] = pick(t, table[other * members + k, 4 + t % 2], True)
        lasts[t].start()
        columns = pl.ds(t * wide, wide)
        for k in range(members):
            got = pick(t, table[me * members + k, 4 + t % 2], True)
            kept = state[k, :, pl.ds(mine, half), columns]
            out[k, :, pl.ds(mine, half), columns] = (
                jnp.where(table[me * members + k, 6] != 0, got, kept) + jitter[k, :, pl.ds(mine, half), columns]
            )
    for t in pieces:
        lasts[t].wait_recv()
        columns = pl.ds(t * wide, wide)
        for k in range(members):
            kept = state[k, :, pl.ds(theirs, half), columns]
            out[k, :, pl.ds(theirs, half), columns] = (
                jnp.where(table[me * members + k, 6] != 0, last_recv[t, k], kept)
                + jitter[k, :, pl.ds(theirs, half), columns]
            )
    for copy in rims:
        copy.wait()
    for copy in cores + firsts + seconds + lasts:
        copy.wait_send()


def resample(number, c1, c2, count, table, state, jitter, depth, coriolis, drag):
    members, parts, rows, width = state.shape
    f32 = jnp.float32
    vmem = pl.BlockSpec(memory_space=pltpu.VMEM)

    def slots(*lead):
        return pltpu.VMEM((*lead, parts, rows // 2, width // PIECES), f32)

    return pl.pallas_call(
        functools.partial(resample_kernel, c1, c2, count),
        out_shape=(
            jax.ShapeDtypeStruct(state.shape, f32), jax.ShapeDtypeStruct((2, 4, width), f32),
        ),
        in_specs=[pl.BlockSpec(memory_space=pltpu.SMEM)] + [vmem] * 5,
        out_specs=(vmem, vmem),
        scratch_shapes=[
            pltpu.VMEM((2, 4, width), f32),
            slots(PIECES, CAP), slots(PIECES, members), slots(PIECES, members),
            [slots(2 * CAP)] * PIECES, [slots(c1)] * PIECES, [slots(c1)] * PIECES,
            [slots(c2)] * PIECES, [slots(c2)] * PIECES,
            pltpu.SemaphoreType.DMA((4 * PIECES,)), pltpu.SemaphoreType.DMA((4 * PIECES,)),
            pltpu.SemaphoreType.DMA((2,)), pltpu.SemaphoreType.DMA((2,)),
        ],
        compiler_params=pltpu.CompilerParams(
            collective_id=number, has_side_effects=True, vmem_limit_bytes=40 * 1024 * 1024
        ),
        name="resample",
    )(table, state, jitter, depth, coriolis, drag)


def routed(count, ancestor, state, jitter, *planes):
    members = state.shape[0]
    part = ancestor.shape[0]
    table, tier = pl.pallas_call(
        functools.partial(routes_kernel, members),
        out_shape=(
            jax.ShapeDtypeStruct((part, 8), jnp.int32), jax.ShapeDtypeStruct((1,), jnp.int32),
        ),
        in_specs=[pl.BlockSpec(memory_space=pltpu.VMEM)],
        out_specs=(pl.BlockSpec(memory_space=pltpu.VMEM), pl.BlockSpec(memory_space=pltpu.SMEM)),
        name="routes",
    )(ancestor[None, :])
    sizes = TIERS + ((2 * CAP, 2 * members),)
    return lax.switch(
        tier[0],
        [functools.partial(resample, 1 + n, c1, c2, count) for n, (c1, c2) in enumerate(sizes)],
        table, state, jitter, *planes,
    )


def edge_rows(count, *planes):
    stacked = jnp.stack(planes + planes[-1:])
    after = [(i, (i + 1) % count) for i in range(count)]
    before = [((i + 1) % count, i) for i in range(count)]
    return jnp.stack(
        [lax.ppermute(stacked[:, -1], "space", after), lax.ppermute(stacked[:, 0], "space", before)]
    )


def gathered(ancestor, state, jitter):
    members = state.shape[0]
    part = ancestor.shape[0]
    first = lax.axis_index("dom") * members
    index = jnp.arange(part, dtype=jnp.int32)
    moved = ancestor != index
    donor = jnp.any((ancestor[:, None] == index[None, :]) & moved[:, None], axis=0)
    earlier = (index[None, :] < index[:, None]) & (index[None, :] // members == index[:, None] // members)
    place = jnp.sum((earlier & donor[None, :]).astype(jnp.int32), axis=1)
    sent = []
    for k in range(CAP):
        hit = donor & (place == k) & (index // members == first // members)
        slot = jnp.sum(jnp.where(hit, index - first, 0))
        sent.append(lax.dynamic_slice_in_dim(state, slot, 1))
    pool = lax.all_gather(jnp.concatenate(sent), "dom", axis=0, tiled=True)
    where = (ancestor // members) * CAP + jnp.sum(
        jnp.where(ancestor[:, None] == index[None, :], place[None, :], 0), axis=1
    )
    copied = []
    for k in range(members):
        j = first + k
        got = lax.dynamic_slice_in_dim(pool, where[j], 1)
        copied.append(jnp.where(moved[j], got, state[k : k + 1]))
    return jnp.concatenate(copied) + jitter


def local(count, doms, ancestor, state, jitter, depth, coriolis, drag):
    members = state.shape[0]
    simple = doms == 8 and members == 4 and state.shape[2] % 16 == 0
    planes = (depth, coriolis, drag)
    if simple:
        fields, rim = routed(count, ancestor, state, jitter, *planes)
    else:
        fields, rim = gathered(ancestor, state, jitter), edge_rows(count, *planes)
    return advance(fields, *planes, rim, count)


def solution(mesh):
    field = P("dom", None, "space", None)
    plane = P("space", None)
    return jax.shard_map(
        functools.partial(local, mesh.shape["space"], mesh.shape["dom"]),
        mesh=mesh,
        in_specs=(P(), field, field, plane, plane, plane),
        out_specs=field,
        check_vma=False,
    )
```

time: 57.8 us -> 55.3 us (0.957)
  local copies, waits for them, and re-layouts: 3.09 us -> 1.15 us
    broadcast_in_dim x1 -> x0, local copies, waits for them, and re-layouts: 1.34 us -> none  [routed(): ancestor[:, None]]
    slice x1 -> x0, local copies, waits for them, and re-layouts: 0.58 us -> none  [routed(): table[CAP, 7]]
    unnamed x7 -> x1, local copies, waits for them, and re-layouts: 1.16 us -> 1.15 us
where the time goes in v3:
time: 55.3 us; the launch traced here: 55.2 us
  Pallas kernels  53.3 us (96%)
  local copies, waits for them, and re-layouts  1.15 us (2%)
  between operations  0.67 us (1%)
    pallas_call x1, Pallas kernels, advance(): pl.pallas_call(functools.partial(advance_kernel, count, groups), out_shap...  27.1 us
    pallas_call x1, Pallas kernels, resample(): pl.pallas_call(functools.partial(resample_kernel, c1, c2, count), out_sha...  24.7 us
    pallas_call x1, Pallas kernels, routed(): pl.pallas_call(functools.partial(routes_kernel, members), out_shape=(jax....  1.5 us
    unnamed x1, local copies, waits for them, and re-layouts  1.15 us

profile of v3, /device:TPU:0, one launch (start us, length us, event | category | flops | bytes accessed | tf_op | source)
XLA Modules:
  0.0 55.2 jit_solution(8064735215896268829)
XLA Ops:
  0.0 1.5 %routes.1 = (s32[32,8]{1,0:T(8,128)S(1)}, s32[1]{0:T(128)}) custom-call(s32[1,32]{1,0:T(1,128)} %bitcast.2), custom_call_target="tpu_custom_call" | custom-call | tf_op jit(solution)/shard_map/routes/pallas_call | solution.py:382
  2.2 24.8 %conditional.1 = ((f32[4,3,16,2048]{3,2,1,0:T(8,128)S(1)}, f32[2,4,2048]{2,1,0:T(4,128)S(1)})) conditional(s32[]{:T(128)} %bitcast.1, (s32[32,8]{1,0:T(8,128)S(1)}, f32[4,3,16,2048]{3,2,1,0:T(8,128)}, f32[4,3,16,2048]{3,2,1,0:T(8,128)}, f32[16,2048]{1,0:T(8,128)}, f32[16,2048]{1,0:T(8,128)}, ...), branch_computations={%region_0.0_spmd, %region_1.0_spmd, %region_2.0_spmd, %region_3.0_... | conditional | bytes 8 | solution.py:392
  2.2 24.7 %resample.5 = (f32[4,3,16,2048]{3,2,1,0:T(8,128)S(1)}, f32[2,4,2048]{2,1,0:T(4,128)S(1)}) custom-call(s32[32,8]{1,0:T(8,128)S(1)} %get-tuple-element.59.table, f32[4,3,16,2048]{3,2,1,0:T(8,128)} %get-tuple-element.60.state, f32[4,3,16,2048]{3,2,1,0:T(8,128)} %get-tuple-element.61.jitter, f32[16,2048]{1,0:T(8,128)} %get-tuple-element.62.depth, ...), custom_call_target="tpu_custom_call" | custom-call | tf_op jit(solution)/shard_map/cond/branch_1_fun/resample/pallas_call | solution.py:357
  26.9 27.1 %advance.1 = f32[4,3,16,2048]{3,2,1,0:T(8,128)S(1)} custom-call(f32[4,3,16,2048]{3,2,1,0:T(8,128)S(1)} %get-tuple-element.83.fields, f32[16,2048]{1,0:T(8,128)} %depth.1, f32[16,2048]{1,0:T(8,128)} %coriolis.1, f32[16,2048]{1,0:T(8,128)} %drag.1, f32[2,4,2048]{2,1,0:T(4,128)S(1)} %get-tuple-element.84.rim), custom_call_target="tpu_custom_call" | custom-call | tf_op jit(solution)/shard_map/advance/pallas_call | solution.py:162
  54.0 1.1 %copy.16 = f32[4,3,16,2048]{3,2,1,0:T(8,128)} copy(f32[4,3,16,2048]{3,2,1,0:T(8,128)S(1)} %advance.1) | data formatting | bytes 3145728

commit v4 on v3

--- a/solution.py
+++ b/solution.py
@@ -14,12 +14,19 @@
 UP, DOWN = 0, 1
 
 
-def column_difference(a, edge):
-    width = a.shape[1]
-    column = lax.broadcasted_iota(jnp.int32, a.shape, 1)
-    beyond = a if edge else jnp.zeros_like(a)
-    after = jnp.where(column == width - 1, beyond, pltpu.roll(a, width - 1, 1))
-    before = jnp.where(column == 0, beyond, pltpu.roll(a, 1, 1))
+def column_difference(load, start, size, width, edge):
+    low, high = max(start - 128, 0), min(start + size + 128, width)
+    a = load(low, high)
+    after = pltpu.roll(a, high - low - 1, 1)[:, start - low : start - low + size]
+    before = pltpu.roll(a, 1, 1)[:, start - low : start - low + size]
+    if low == start or high == start + size:
+        here = a[:, start - low : start - low + size]
+        beyond = here if edge else jnp.zeros_like(here)
+        column = lax.broadcasted_iota(jnp.int32, here.shape, 1)
+        if high == start + size:
+            after = jnp.where(column == size - 1, beyond, after)
+        if low == start:
+            before = jnp.where(column == 0, beyond, before)
     return after - before
 
 
@@ -88,63 +95,83 @@
             rim_c[3, at, :] = 0.5 * DT * k
             rim_c[4, at, :] = 0.5 * DT * k if side == UP else -0.5 * DT * k
 
-    def finish(step, group):
+    chunk = min(512, width)
+    chunks = [(start, pl.ds(start, chunk)) for start in range(0, width, chunk)]
+
+    def arrived(step, group):
         for side in (UP, DOWN):
             swap(step, group, side).wait_recv()
-        come = last_recv.at[group] if step == STEPS else recv.at[step, group]
-        if step < STEPS:
-            for side in (UP, DOWN):
-                at = slice(side * each, (side + 1) * each)
-                near[at, :] = come[side, 0:each, :]
-                far[at, :] = send[step, group, side, 0:each, :] - come[side, each : 2 * each, :]
-            u, v = halo[group, 0], halo[group, 1]
-            halo[group, 0] = u * rim_c[1] + v * rim_c[2] - rim_c[3] * column_difference(near[...], True)
-            halo[group, 1] = v * rim_c[1] - u * rim_c[2] - rim_c[4] * far[...]
-        for i in range(each):
-            p = group * each + i
-            out[p, 2] = out[p, 2] - push_c[...] * row_difference(
-                out[p, 0], come[UP, i : i + 1, :], come[DOWN, i : i + 1, :]
-            )
+        return last_recv.at[group] if step == STEPS else recv.at[step, group]
+
+    def beside(step, group, come):
+        for side in (UP, DOWN):
+            at = slice(side * each, (side + 1) * each)
+            near[at, :] = come[side, 0:each, :]
+            far[at, :] = send[step, group, side, 0:each, :] - come[side, each : 2 * each, :]
+        u, v = halo[group, 0], halo[group, 1]
+        slope = column_difference(lambda low, high: near[:, low:high], 0, width, width, True)
+        halo[group, 0] = u * rim_c[1] + v * rim_c[2] - rim_c[3] * slope
+        halo[group, 1] = v * rim_c[1] - u * rim_c[2] - rim_c[4] * far[...]
+
+    def along(p, i, come, at):
+        return out[p, 2, :, at] - push_c[:, at] * row_difference(
+            out[p, 0, :, at], come[UP, i : i + 1, at], come[DOWN, i : i + 1, at]
+        )
 
     for step in range(1, STEPS + 1):
         old = fields if step == 1 else out
         for group in range(groups):
+            come = arrived(step - 1, group)
             if step == 1:
                 for side in (UP, DOWN):
-                    swap(0, group, side).wait_recv()
-                for side in (UP, DOWN):
                     for k in range(2):
-                        halo[group, k, side * each : (side + 1) * each, :] = recv[
-                            0, group, side, k * each : (k + 1) * each, :
+                        halo[group, k, side * each : (side + 1) * each, :] = come[
+                            side, k * each : (k + 1) * each, :
                         ]
             else:
-                finish(step - 1, group)
+                beside(step - 1, group, come)
             near[...] = rim_c[0] * halo[group, 1]
             for i in range(each):
                 p = group * each + i
-                f = flux_c[...]
-                height = old[p, 0] - (
-                    column_difference(f * old[p, 1], False)
-                    + row_difference(f * old[p, 2], near[i : i + 1, :], near[each + i : each + i + 1, :])
-                )
-                out[p, 0] = height
-                if step == STEPS:
-                    last_send[group, UP, i : i + 1, :] = height[0:1, :]
-                    last_send[group, DOWN, i : i + 1, :] = height[rows - 1 : rows, :]
-                else:
-                    for k in range(2):
-                        at = slice(k * each + i, k * each + i + 1)
-                        send[step, group, UP, at, :] = height[k : k + 1, :]
-                        send[step, group, DOWN, at, :] = height[rows - 1 - k : rows - k, :]
+                for start, at in chunks:
+                    if step == 1:
+                        v = fields[p, 2, :, at]
+                    else:
+                        v = along(p, i, come, at)
+                        out[p, 2, :, at] = v
+                    outflow = column_difference(
+                        lambda low, high: flux_c[:, low:high] * old[p, 1, :, low:high], start, chunk, width, False
+                    )
+                    height = old[p, 0, :, at] - (
+                        outflow
+                        + row_difference(flux_c[:, at] * v, near[i : i + 1, at], near[each + i : each + i + 1, at])
+                    )
+                    out[p, 0, :, at] = height
+                    if step == STEPS:
+                        last_send[group, UP, i : i + 1, at] = height[0:1, :]
+                        last_send[group, DOWN, i : i + 1, at] = height[rows - 1 : rows, :]
+                    else:
+                        for k in range(2):
+                            n = k * each + i
+                            send[step, group, UP, n : n + 1, at] = height[k : k + 1, :]
+                            send[step, group, DOWN, n : n + 1, at] = height[rows - 1 - k : rows - k, :]
             for side in (UP, DOWN):
                 swap(step, group, side).start()
             for i in range(each):
                 p = group * each + i
-                u, v = old[p, 1], old[p, 2]
-                out[p, 1] = u * keep_c[...] + turn_c[...] * v - push_c[...] * column_difference(out[p, 0], True)
-                out[p, 2] = v * keep_c[...] - turn_c[...] * u
+                for start, at in chunks:
+                    u, v = old[p, 1, :, at], (old if step == 1 else out)[p, 2, :, at]
+                    slope = column_difference(
+                        lambda low, high: out[p, 0, :, low:high], start, chunk, width, True
+                    )
+                    out[p, 1, :, at] = u * keep_c[:, at] + turn_c[:, at] * v - push_c[:, at] * slope
+                    out[p, 2, :, at] = v * keep_c[:, at] - turn_c[:, at] * u
     for group in range(groups):
-        finish(STEPS, group)
+        come = arrived(STEPS, group)
+        for i in range(each):
+            p = group * each + i
+            for start, at in chunks:
+                out[p, 2, :, at] = along(p, i, come, at)
     for step in range(STEPS + 1):
         for group in range(groups):
             for side in (UP, DOWN):

time: 55.3 us -> 55.3 us (level)
  no operation moved by 1% of the time
where the time goes in v4:
time: 55.3 us; the launch traced here: 55.2 us
  Pallas kernels  53.3 us (96%)
  local copies, waits for them, and re-layouts  1.15 us (2%)
  between operations  0.67 us (1%)
    pallas_call x1, Pallas kernels, advance(): pl.pallas_call(functools.partial(advance_kernel, count, groups), out_shap...  27.1 us
    pallas_call x1, Pallas kernels, resample(): pl.pallas_call(functools.partial(resample_kernel, c1, c2, count), out_sha...  24.7 us
    pallas_call x1, Pallas kernels, routed(): pl.pallas_call(functools.partial(routes_kernel, members), out_shape=(jax....  1.5 us
    unnamed x1, local copies, waits for them, and re-layouts  1.15 us

profile of v4, /device:TPU:0, one launch (start us, length us, event | category | flops | bytes accessed | tf_op | source)
XLA Modules:
  0.0 55.2 jit_solution(17866053402027401980)
XLA Ops:
  0.0 1.5 %routes.1 = (s32[32,8]{1,0:T(8,128)S(1)}, s32[1]{0:T(128)}) custom-call(s32[1,32]{1,0:T(1,128)} %bitcast.2), custom_call_target="tpu_custom_call" | custom-call | tf_op jit(solution)/shard_map/routes/pallas_call | solution.py:409
  2.2 24.8 %conditional.1 = ((f32[4,3,16,2048]{3,2,1,0:T(8,128)S(1)}, f32[2,4,2048]{2,1,0:T(4,128)S(1)})) conditional(s32[]{:T(128)} %bitcast.1, (s32[32,8]{1,0:T(8,128)S(1)}, f32[4,3,16,2048]{3,2,1,0:T(8,128)}, f32[4,3,16,2048]{3,2,1,0:T(8,128)}, f32[16,2048]{1,0:T(8,128)}, f32[16,2048]{1,0:T(8,128)}, ...), branch_computations={%region_0.0_spmd, %region_1.0_spmd, %region_2.0_spmd, %region_3.0_... | conditional | bytes 8 | solution.py:419
  2.2 24.7 %resample.5 = (f32[4,3,16,2048]{3,2,1,0:T(8,128)S(1)}, f32[2,4,2048]{2,1,0:T(4,128)S(1)}) custom-call(s32[32,8]{1,0:T(8,128)S(1)} %get-tuple-element.59.table, f32[4,3,16,2048]{3,2,1,0:T(8,128)} %get-tuple-element.60.state, f32[4,3,16,2048]{3,2,1,0:T(8,128)} %get-tuple-element.61.jitter, f32[16,2048]{1,0:T(8,128)} %get-tuple-element.62.depth, ...), custom_call_target="tpu_custom_call" | custom-call | tf_op jit(solution)/shard_map/cond/branch_1_fun/resample/pallas_call | solution.py:384
  26.9 27.1 %advance.1 = f32[4,3,16,2048]{3,2,1,0:T(8,128)S(1)} custom-call(f32[4,3,16,2048]{3,2,1,0:T(8,128)S(1)} %get-tuple-element.83.fields, f32[16,2048]{1,0:T(8,128)} %depth.1, f32[16,2048]{1,0:T(8,128)} %coriolis.1, f32[16,2048]{1,0:T(8,128)} %drag.1, f32[2,4,2048]{2,1,0:T(4,128)S(1)} %get-tuple-element.84.rim), custom_call_target="tpu_custom_call" | custom-call | tf_op jit(solution)/shard_map/advance/pallas_call | solution.py:189
  54.0 1.1 %copy.16 = f32[4,3,16,2048]{3,2,1,0:T(8,128)} copy(f32[4,3,16,2048]{3,2,1,0:T(8,128)S(1)} %advance.1) | data formatting | bytes 3145728

commit v5 on v4

--- a/solution.py
+++ b/solution.py
@@ -180,7 +180,7 @@
 
 def advance(fields, depth, coriolis, drag, rim, count):
     members, _, rows, width = fields.shape
-    groups = 2
+    groups = members
     each = members // groups
     f32 = jnp.float32
     plane = pltpu.VMEM((rows, width), f32)

time: 55.3 us -> 54.2 us (0.980)
  Pallas kernels: 53.3 us -> 52.2 us
    pallas_call x1, Pallas kernels: 27.1 us -> 26 us  [advance(): pl.pallas_call(functools.partial(advance_kernel, count, groups), out_shap...]
where the time goes in v5:
time: 54.2 us; the launch traced here: 54 us
  Pallas kernels  52.2 us (96%)
  local copies, waits for them, and re-layouts  1.15 us (2%)
  between operations  0.67 us (1%)
    pallas_call x1, Pallas kernels, advance(): pl.pallas_call(functools.partial(advance_kernel, count, groups), out_shap...  26 us
    pallas_call x1, Pallas kernels, resample(): pl.pallas_call(functools.partial(resample_kernel, c1, c2, count), out_sha...  24.7 us
    pallas_call x1, Pallas kernels, routed(): pl.pallas_call(functools.partial(routes_kernel, members), out_shape=(jax....  1.5 us
    unnamed x1, local copies, waits for them, and re-layouts  1.15 us

profile of v5, /device:TPU:0, one launch (start us, length us, event | category | flops | bytes accessed | tf_op | source)
XLA Modules:
  0.0 54.0 jit_solution(74148831984409248)
XLA Ops:
  0.0 1.5 %routes.1 = (s32[32,8]{1,0:T(8,128)S(1)}, s32[1]{0:T(128)}) custom-call(s32[1,32]{1,0:T(1,128)} %bitcast.2), custom_call_target="tpu_custom_call" | custom-call | tf_op jit(solution)/shard_map/routes/pallas_call | solution.py:409
  2.2 24.8 %conditional.1 = ((f32[4,3,16,2048]{3,2,1,0:T(8,128)S(1)}, f32[2,4,2048]{2,1,0:T(4,128)S(1)})) conditional(s32[]{:T(128)} %bitcast.1, (s32[32,8]{1,0:T(8,128)S(1)}, f32[4,3,16,2048]{3,2,1,0:T(8,128)}, f32[4,3,16,2048]{3,2,1,0:T(8,128)}, f32[16,2048]{1,0:T(8,128)}, f32[16,2048]{1,0:T(8,128)}, ...), branch_computations={%region_0.0_spmd, %region_1.0_spmd, %region_2.0_spmd, %region_3.0_... | conditional | bytes 8 | solution.py:419
  2.2 24.7 %resample.5 = (f32[4,3,16,2048]{3,2,1,0:T(8,128)S(1)}, f32[2,4,2048]{2,1,0:T(4,128)S(1)}) custom-call(s32[32,8]{1,0:T(8,128)S(1)} %get-tuple-element.59.table, f32[4,3,16,2048]{3,2,1,0:T(8,128)} %get-tuple-element.60.state, f32[4,3,16,2048]{3,2,1,0:T(8,128)} %get-tuple-element.61.jitter, f32[16,2048]{1,0:T(8,128)} %get-tuple-element.62.depth, ...), custom_call_target="tpu_custom_call" | custom-call | tf_op jit(solution)/shard_map/cond/branch_1_fun/resample/pallas_call | solution.py:384
  26.9 26.0 %advance.1 = f32[4,3,16,2048]{3,2,1,0:T(8,128)S(1)} custom-call(f32[4,3,16,2048]{3,2,1,0:T(8,128)S(1)} %get-tuple-element.83.fields, f32[16,2048]{1,0:T(8,128)} %depth.1, f32[16,2048]{1,0:T(8,128)} %coriolis.1, f32[16,2048]{1,0:T(8,128)} %drag.1, f32[2,4,2048]{2,1,0:T(4,128)S(1)} %get-tuple-element.84.rim), custom_call_target="tpu_custom_call" | custom-call | tf_op jit(solution)/shard_map/advance/pallas_call | solution.py:189
  52.9 1.1 %copy.16 = f32[4,3,16,2048]{3,2,1,0:T(8,128)} copy(f32[4,3,16,2048]{3,2,1,0:T(8,128)S(1)} %advance.1) | data formatting | bytes 3145728

commit v6 on v5

--- a/solution.py
+++ b/solution.py
@@ -46,7 +46,7 @@
 
 
 def advance_kernel(
-    count, groups,
+    count, groups, greet,
     fields, depth, coriolis, drag, rim, out,
     flux_c, keep_c, turn_c, push_c, rim_c, send, recv, last_send, last_recv, halo, near, far,
     send_sem, recv_sem,
@@ -56,9 +56,10 @@
     me = lax.axis_index("space")
     towards = (lax.rem(me + count - 1, count), lax.rem(me + 1, count))
 
-    barrier = pltpu.get_barrier_semaphore()
-    for neighbour in towards:
-        pl.semaphore_signal(barrier, inc=1, device_id={"space": neighbour}, device_id_type=MESH)
+    if greet:
+        barrier = pltpu.get_barrier_semaphore()
+        for neighbour in towards:
+            pl.semaphore_signal(barrier, inc=1, device_id={"space": neighbour}, device_id_type=MESH)
 
     def swap(step, group, side):
         number = 2 * (step * groups + group) + side
@@ -74,7 +75,8 @@
                 for k in range(2):
                     at = slice(k * each + i, k * each + i + 1)
                     send[0, group, side, at, :] = fields[group * each + i, 1 + k, row : row + 1, :]
-    pl.semaphore_wait(barrier, 2)
+    if greet:
+        pl.semaphore_wait(barrier, 2)
     for group in range(groups):
         for side in (UP, DOWN):
             swap(0, group, side).start()
@@ -178,31 +180,35 @@
                 swap(step, group, side).wait_send()
 
 
-def advance(fields, depth, coriolis, drag, rim, count):
-    members, _, rows, width = fields.shape
-    groups = members
+def advance_scratch(members, rows, width, groups):
     each = members // groups
     f32 = jnp.float32
     plane = pltpu.VMEM((rows, width), f32)
     edges = pltpu.VMEM((2 * each, width), f32)
     copies = 2 * (STEPS + 1) * groups
+    return [
+        plane, plane, plane, plane,
+        pltpu.VMEM((5, 2 * each, width), f32),
+        pltpu.VMEM((STEPS, groups, 2, 2 * each, width), f32),
+        pltpu.VMEM((STEPS, groups, 2, 2 * each, width), f32),
+        pltpu.VMEM((groups, 2, each, width), f32),
+        pltpu.VMEM((groups, 2, each, width), f32),
+        pltpu.VMEM((groups, 2, 2 * each, width), f32),
+        edges, edges,
+        pltpu.SemaphoreType.DMA((copies,)),
+        pltpu.SemaphoreType.DMA((copies,)),
+    ]
+
+
+def advance(fields, depth, coriolis, drag, rim, count):
+    members, _, rows, width = fields.shape
+    groups = members
     return pl.pallas_call(
-        functools.partial(advance_kernel, count, groups),
-        out_shape=jax.ShapeDtypeStruct(fields.shape, f32),
+        functools.partial(advance_kernel, count, groups, True),
+        out_shape=jax.ShapeDtypeStruct(fields.shape, jnp.float32),
         in_specs=[pl.BlockSpec(memory_space=pltpu.VMEM)] * 5,
         out_specs=pl.BlockSpec(memory_space=pltpu.VMEM),
-        scratch_shapes=[
-            plane, plane, plane, plane,
-            pltpu.VMEM((5, 2 * each, width), f32),
-            pltpu.VMEM((STEPS, groups, 2, 2 * each, width), f32),
-            pltpu.VMEM((STEPS, groups, 2, 2 * each, width), f32),
-            pltpu.VMEM((groups, 2, each, width), f32),
-            pltpu.VMEM((groups, 2, each, width), f32),
-            pltpu.VMEM((groups, 2, 2 * each, width), f32),
-            edges, edges,
-            pltpu.SemaphoreType.DMA((copies,)),
-            pltpu.SemaphoreType.DMA((copies,)),
-        ],
+        scratch_shapes=advance_scratch(members, rows, width, groups),
         compiler_params=pltpu.CompilerParams(
             collective_id=0, has_side_effects=True, vmem_limit_bytes=40 * 1024 * 1024
         ),
@@ -268,7 +274,7 @@
         out[:, k : k + 1] = columns[k]
 
 
-TIERS = ((2, 2), (3, 3), (4, 4))
+TIERS = ((3, 3), (4, 4))
 PIECES = 4
 
 
@@ -373,8 +379,15 @@
         copy.wait_send()
 
 
-def resample(number, c1, c2, count, table, state, jitter, depth, coriolis, drag):
+def cycle_kernel(c1, c2, count, groups, table, state, jitter, depth, coriolis, drag, out, rim, *scratch):
+    first = len(scratch) - len(advance_scratch(4, 16, 2048, groups))
+    resample_kernel(c1, c2, count, table, state, jitter, depth, coriolis, drag, out, rim, *scratch[:first])
+    advance_kernel(count, groups, False, out, depth, coriolis, drag, rim, out, *scratch[first:])
+
+
+def cycle(number, c1, c2, count, table, state, jitter, depth, coriolis, drag):
     members, parts, rows, width = state.shape
+    groups = members
     f32 = jnp.float32
     vmem = pl.BlockSpec(memory_space=pltpu.VMEM)
 
@@ -382,24 +395,24 @@
         return pltpu.VMEM((*lead, parts, rows // 2, width // PIECES), f32)
 
     return pl.pallas_call(
-        functools.partial(resample_kernel, c1, c2, count),
-        out_shape=(
-            jax.ShapeDtypeStruct(state.shape, f32), jax.ShapeDtypeStruct((2, 4, width), f32),
-        ),
+        functools.partial(cycle_kernel, c1, c2, count, groups),
+        out_shape=jax.ShapeDtypeStruct(state.shape, f32),
         in_specs=[pl.BlockSpec(memory_space=pltpu.SMEM)] + [vmem] * 5,
-        out_specs=(vmem, vmem),
+        out_specs=vmem,
         scratch_shapes=[
+            pltpu.VMEM((2, 4, width), f32),
             pltpu.VMEM((2, 4, width), f32),
             slots(PIECES, CAP), slots(PIECES, members), slots(PIECES, members),
             [slots(2 * CAP)] * PIECES, [slots(c1)] * PIECES, [slots(c1)] * PIECES,
             [slots(c2)] * PIECES, [slots(c2)] * PIECES,
             pltpu.SemaphoreType.DMA((4 * PIECES,)), pltpu.SemaphoreType.DMA((4 * PIECES,)),
             pltpu.SemaphoreType.DMA((2,)), pltpu.SemaphoreType.DMA((2,)),
-        ],
+        ]
+        + advance_scratch(members, rows, width, groups),
         compiler_params=pltpu.CompilerParams(
             collective_id=number, has_side_effects=True, vmem_limit_bytes=40 * 1024 * 1024
         ),
-        name="resample",
+        name="cycle",
     )(table, state, jitter, depth, coriolis, drag)
 
 
@@ -418,7 +431,7 @@
     sizes = TIERS + ((2 * CAP, 2 * members),)
     return lax.switch(
         tier[0],
-        [functools.partial(resample, 1 + n, c1, c2, count) for n, (c1, c2) in enumerate(sizes)],
+        [functools.partial(cycle, 1 + n, c1, c2, count) for n, (c1, c2) in enumerate(sizes)],
         table, state, jitter, *planes,
     )
 
@@ -463,10 +476,8 @@
     simple = doms == 8 and members == 4 and state.shape[2] % 16 == 0
     planes = (depth, coriolis, drag)
     if simple:
-        fields, rim = routed(count, ancestor, state, jitter, *planes)
-    else:
-        fields, rim = gathered(ancestor, state, jitter), edge_rows(count, *planes)
-    return advance(fields, *planes, rim, count)
+        return routed(count, ancestor, state, jitter, *planes)
+    return advance(gathered(ancestor, state, jitter), *planes, edge_rows(count, *planes), count)
 
 
 def solution(mesh):

time: 54.2 us -> 51 us (0.941)
  Pallas kernels: 52.2 us -> 48.8 us
    pallas_call x2 -> x1, Pallas kernels: 50.7 us -> 47.3 us  [cycle(): pl.pallas_call(functools.partial(cycle_kernel, c1, c2, count, groups), ou...]
where the time goes in v6:
time: 51 us; the launch traced here: 50.8 us
  Pallas kernels  48.8 us (96%)
  local copies, waits for them, and re-layouts  1.15 us (2%)
  between operations  0.67 us (1%)
    pallas_call x1, Pallas kernels, cycle(): pl.pallas_call(functools.partial(cycle_kernel, c1, c2, count, groups), ou...  47.3 us
    pallas_call x1, Pallas kernels, routed(): pl.pallas_call(functools.partial(routes_kernel, members), out_shape=(jax....  1.5 us
    unnamed x1, local copies, waits for them, and re-layouts  1.15 us

profile of v6, /device:TPU:0, one launch (start us, length us, event | category | flops | bytes accessed | tf_op | source)
XLA Modules:
  0.0 50.8 jit_solution(14702258038737649294)
XLA Ops:
  0.0 1.5 %routes.1 = (s32[32,8]{1,0:T(8,128)S(1)}, s32[1]{0:T(128)}) custom-call(s32[1,32]{1,0:T(1,128)} %bitcast.2), custom_call_target="tpu_custom_call" | custom-call | tf_op jit(solution)/shard_map/routes/pallas_call | solution.py:422
  2.2 47.5 %conditional.1 = (f32[4,3,16,2048]{3,2,1,0:T(8,128)S(1)}) conditional(s32[]{:T(128)} %bitcast.1, (s32[32,8]{1,0:T(8,128)S(1)}, f32[4,3,16,2048]{3,2,1,0:T(8,128)}, f32[4,3,16,2048]{3,2,1,0:T(8,128)}, f32[16,2048]{1,0:T(8,128)}, f32[16,2048]{1,0:T(8,128)}, /*index=5*/f32[16,2048]{1,0:T(8,128)}) %tuple.14, (s32[32,8]{1,0:T(8,128)S(1)}, ...), branch_computations={%region_0.0_spmd, %region_1.0_spmd, %region_2.0_spmd} | conditional | bytes 8 | solution.py:432
  2.2 47.3 %cycle.3 = f32[4,3,16,2048]{3,2,1,0:T(8,128)S(1)} custom-call(s32[32,8]{1,0:T(8,128)S(1)} %get-tuple-element.44.table, f32[4,3,16,2048]{3,2,1,0:T(8,128)} %get-tuple-element.46.state, f32[4,3,16,2048]{3,2,1,0:T(8,128)} %get-tuple-element.47.jitter, f32[16,2048]{1,0:T(8,128)} %get-tuple-element.48.depth, f32[16,2048]{1,0:T(8,128)} %get-tuple-element.49.coriolis, ...), custom_call_target="tpu_custom_call" | custom-call | tf_op jit(solution)/shard_map/cond/branch_0_fun/cycle/pallas_call | solution.py:397
  49.7 1.1 %copy.14 = f32[4,3,16,2048]{3,2,1,0:T(8,128)} copy(f32[4,3,16,2048]{3,2,1,0:T(8,128)S(1)} %get-tuple-element.67) | data formatting | bytes 3145728

commit v7 on v6

--- a/solution.py
+++ b/solution.py
@@ -122,7 +122,7 @@
 
     for step in range(1, STEPS + 1):
         old = fields if step == 1 else out
-        for group in range(groups):
+        def forward(group, carry, step=step, old=old):
             come = arrived(step - 1, group)
             if step == 1:
                 for side in (UP, DOWN):
@@ -168,12 +168,19 @@
                     )
                     out[p, 1, :, at] = u * keep_c[:, at] + turn_c[:, at] * v - push_c[:, at] * slope
                     out[p, 2, :, at] = v * keep_c[:, at] - turn_c[:, at] * u
-    for group in range(groups):
+            return carry
+
+        lax.fori_loop(0, groups, forward, 0)
+
+    def close(group, carry):
         come = arrived(STEPS, group)
         for i in range(each):
             p = group * each + i
             for start, at in chunks:
                 out[p, 2, :, at] = along(p, i, come, at)
+        return carry
+
+    lax.fori_loop(0, groups, close, 0)
     for step in range(STEPS + 1):
         for group in range(groups):
             for side in (UP, DOWN):

time: 51 us -> 50.7 us (level)
  no operation moved by 1% of the time
where the time goes in v7:
time: 50.7 us; the launch traced here: 50.6 us
  Pallas kernels  48.8 us (96%)
  local copies, waits for them, and re-layouts  1.15 us (2%)
  between operations  0.67 us (1%)
    pallas_call x1, Pallas kernels, cycle(): pl.pallas_call(functools.partial(cycle_kernel, c1, c2, count, groups), ou...  47.3 us
    pallas_call x1, Pallas kernels, routed(): pl.pallas_call(functools.partial(routes_kernel, members), out_shape=(jax....  1.5 us
    unnamed x1, local copies, waits for them, and re-layouts  1.15 us

profile of v7, /device:TPU:0, one launch (start us, length us, event | category | flops | bytes accessed | tf_op | source)
XLA Modules:
  0.0 50.6 jit_solution(17448887915783383893)
XLA Ops:
  0.0 1.5 %routes.1 = (s32[32,8]{1,0:T(8,128)S(1)}, s32[1]{0:T(128)}) custom-call(s32[1,32]{1,0:T(1,128)} %bitcast.2), custom_call_target="tpu_custom_call" | custom-call | tf_op jit(solution)/shard_map/routes/pallas_call | solution.py:429
  2.2 47.3 %conditional.1 = (f32[4,3,16,2048]{3,2,1,0:T(8,128)S(1)}) conditional(s32[]{:T(128)} %bitcast.1, (s32[32,8]{1,0:T(8,128)S(1)}, f32[4,3,16,2048]{3,2,1,0:T(8,128)}, f32[4,3,16,2048]{3,2,1,0:T(8,128)}, f32[16,2048]{1,0:T(8,128)}, f32[16,2048]{1,0:T(8,128)}, /*index=5*/f32[16,2048]{1,0:T(8,128)}) %tuple.14, (s32[32,8]{1,0:T(8,128)S(1)}, ...), branch_computations={%region_0.0_spmd, %region_1.0_spmd, %region_2.0_spmd} | conditional | bytes 8 | solution.py:439
  2.2 47.3 %cycle.3 = f32[4,3,16,2048]{3,2,1,0:T(8,128)S(1)} custom-call(s32[32,8]{1,0:T(8,128)S(1)} %get-tuple-element.44.table, f32[4,3,16,2048]{3,2,1,0:T(8,128)} %get-tuple-element.46.state, f32[4,3,16,2048]{3,2,1,0:T(8,128)} %get-tuple-element.47.jitter, f32[16,2048]{1,0:T(8,128)} %get-tuple-element.48.depth, f32[16,2048]{1,0:T(8,128)} %get-tuple-element.49.coriolis, ...), custom_call_target="tpu_custom_call" | custom-call | tf_op jit(solution)/shard_map/cond/branch_0_fun/cycle/pallas_call | solution.py:404
  49.4 1.1 %copy.14 = f32[4,3,16,2048]{3,2,1,0:T(8,128)} copy(f32[4,3,16,2048]{3,2,1,0:T(8,128)S(1)} %get-tuple-element.67) | data formatting | bytes 3145728
